TPU v7x, 32 devices: a whole 2x2x4 slice. The times are simulated.
32 devices in a mesh: det: 4 (over z), tm: 8 (over y, x, core).
Axes of the slice: x: 2, y: 2, z: 4, core: 2. Of those that a mesh axis runs over, the one named last changes fastest.
Arguments:
- iterate: float32 [16, 262144], P(None, ('det', 'tm')), may hold values from -6 to 6
- residual: float32 [16, 262144], P(None, ('det', 'tm')), may hold values from -40 to 40
- direction: float32 [16, 262144], P(None, ('det', 'tm')), may hold values from -2.5 to 2.5
- precond: float32 [262144], P(('det', 'tm')), may hold values from 0.02 to 0.12
- patch_ids: int32 [128, 64], P('det', 'tm'), may hold values from 0 to 4095, as said below
- pixel_in: int32 [128, 8192], P('det', 'tm'), may hold values from 0 to 63
- weights: float32 [128, 8192], P('det', 'tm'), may hold values from 0.5 to 1.5
- filter_diag: float32 [128], P('det'), may hold values from 1 to 1.5
- filter_band: float32 [128, 64], P('det'), may hold values from 0.003125 to 0.0075
Outputs:
- new_iterate: float32 [16, 262144], P(None, ('det', 'tm'))
- new_residual: float32 [16, 262144], P(None, ('det', 'tm'))
- new_direction: float32 [16, 262144], P(None, ('det', 'tm'))
Inputs may be any that keep to these rules, and one draw needn't show every extreme that they name: `patch_ids`: the blocks of one device (detectors 32 d0 .. and time blocks 8 t0 .. of its det index a and tm index c) name, for every owner o = a2 * 8 + c2, exactly 8 patches p with p // 128 = o.
All inputs are finite; a program needn't handle non-finite values.
Results may differ from a plain program's by a relative error of at most 0.0003.
Values sent between devices are 32-bit elements; how exact they have to be, the bound alone decides.
A program may use at most 64 MiB of HBM per device.

v0:
```python
import jax
import jax.numpy as jnp
from jax import lax
from jax.sharding import PartitionSpec as P

PX = 64


def with_halo(cells, sides, width):
    for axis, dim in sides:
        count = lax.axis_size(axis)
        ends = count - 1
        head = lax.slice_in_dim(cells, 0, width, axis=dim)
        tail = lax.slice_in_dim(cells, cells.shape[dim] - width, cells.shape[dim], axis=dim)
        cells = jnp.concatenate(
            [
                lax.ppermute(tail, axis, [(i, (i + 1) % count) for i in range(ends)]),
                cells,
                lax.ppermute(head, axis, [((i + 1) % count, i) for i in range(ends)]),
            ],
            axis=dim,
        )
    return cells


def per_device(
    iterate, residual, direction, precond, patch_ids, pixel_in, weights, filter_diag, filter_band
):
    probes = iterate.shape[0]
    det_rows, time_blocks = patch_ids.shape
    samples = pixel_in.shape[1]
    block_len = samples // time_blocks
    half_band = filter_band.shape[1]
    groups = lax.axis_size("det")
    spans = lax.axis_size("tm")
    devices = groups * spans
    blocks = det_rows * time_blocks
    per_owner = blocks // devices
    own_patches = iterate.shape[1] // PX
    width = probes * PX
    local_old = jnp.sum(residual * precond * residual, axis=1)
    norm_old = lax.psum(local_old, ("det", "tm"))
    patch_flat = patch_ids.reshape(blocks)
    owners = patch_flat // own_patches
    sort_order = jnp.argsort(owners, stable=True)
    inverse = jnp.argsort(sort_order, stable=True)
    requests = (patch_flat[sort_order] % own_patches).reshape(devices, per_owner)
    asked_rows = lax.all_to_all(requests, ("det", "tm"), split_axis=0, concat_axis=0, tiled=True)
    asked_hot = (
        asked_rows.reshape(-1)[:, None] == jnp.arange(own_patches, dtype=jnp.int32)[None, :]
    ).astype(jnp.float32)
    patch_table = (
        direction.reshape(probes, own_patches, PX).transpose(1, 0, 2).reshape(own_patches, width)
    )
    served = jnp.dot(asked_hot, patch_table, precision=lax.Precision.HIGHEST).reshape(
        devices, per_owner, width
    )
    fetched = lax.all_to_all(served, ("det", "tm"), split_axis=0, concat_axis=0, tiled=True)
    block_vals = fetched.reshape(blocks, width)[inverse].reshape(blocks, probes, PX)
    pixel_hot = (
        pixel_in.reshape(blocks, block_len)[:, :, None]
        == jnp.arange(PX, dtype=jnp.int32)[None, None, :]
    ).astype(jnp.float32)
    sample_gain = weights.reshape(blocks, block_len)
    timeline = (
        jnp.einsum("bpx,bsx->bps", block_vals, pixel_hot, precision=lax.Precision.HIGHEST)
        * sample_gain[:, None, :]
    )
    timeline = (
        timeline.reshape(det_rows, time_blocks, probes, block_len)
        .transpose(2, 0, 1, 3)
        .reshape(probes, det_rows, samples)
    )
    padded = with_halo(timeline, (("tm", 2),), half_band)
    windows = jnp.concatenate(
        [
            padded[:, :, :samples].reshape(probes, det_rows, time_blocks, block_len),
            padded[:, :, block_len : samples + block_len].reshape(
                probes, det_rows, time_blocks, block_len
            ),
        ],
        axis=3,
    )
    coeffs = jnp.concatenate([filter_diag[:, None], filter_band], axis=1)
    offsets = jnp.abs(
        jnp.arange(2 * block_len, dtype=jnp.int32)[:, None]
        - jnp.arange(block_len, dtype=jnp.int32)[None, :]
        - half_band
    )
    band_hot = (
        offsets[:, :, None] == jnp.arange(half_band + 1, dtype=jnp.int32)[None, None, :]
    ).astype(jnp.float32)
    toeplitz = jnp.einsum("usk,dk->dus", band_hot, coeffs, precision=lax.Precision.HIGHEST)
    filtered = jnp.einsum("pdju,dus->pdjs", windows, toeplitz, precision=lax.Precision.HIGHEST)
    weighted = (
        filtered.transpose(1, 2, 0, 3).reshape(blocks, probes, block_len) * sample_gain[:, None, :]
    )
    partial_value = jnp.einsum(
        "bps,bsx->bpx", weighted, pixel_hot, precision=lax.Precision.HIGHEST
    ).reshape(blocks, width)
    partial_value = partial_value[sort_order].reshape(devices, per_owner, width)
    collected = lax.all_to_all(
        partial_value, ("det", "tm"), split_axis=0, concat_axis=0, tiled=True
    )
    collected = collected.reshape(devices * per_owner, width)
    summed = lax.dot_general(
        asked_hot, collected, (((0,), (0,)), ((), ())), precision=lax.Precision.HIGHEST
    )
    image_map = (
        summed.reshape(own_patches, probes, PX).transpose(1, 0, 2).reshape(probes, own_patches * PX)
    )
    local_curv = jnp.sum(direction * image_map, axis=1)
    curvature = lax.psum(local_curv, ("det", "tm"))
    step_size = norm_old / curvature
    new_iterate = iterate + step_size[:, None] * direction
    new_residual = residual - step_size[:, None] * image_map
    scaled = precond * new_residual
    norm_new = lax.psum(jnp.sum(new_residual * scaled, axis=1), ("det", "tm"))
    new_direction = scaled + (norm_new / norm_old)[:, None] * direction
    return (new_iterate, new_residual, new_direction)


def solution(mesh):
    in_specs = (
        P(None, ("det", "tm")),
        P(None, ("det", "tm")),
        P(None, ("det", "tm")),
        P(("det", "tm")),
        P("det", "tm"),
        P("det", "tm"),
        P("det", "tm"),
        P("det"),
        P("det", None),
    )
    out_specs = (P(None, ("det", "tm")), P(None, ("det", "tm")), P(None, ("det", "tm")))
    return jax.shard_map(
        per_device, mesh=mesh, in_specs=in_specs, out_specs=out_specs, check_vma=False
    )
```

profile of v0, /device:TPU:0, one launch (start us, length us, event | category | flops | bytes accessed | tf_op | source)
XLA Modules:
  0.0 209.9 jit_solution(2585544996662870150)
XLA Ops:
  1.5 3.2 %sort.31 = (s32[256]{0:T(256)}, s32[256]{0:T(256)S(1)}) sort(s32[256]{0:T(256)S(1)} %and_select_fusion, s32[256]{0:T(256)S(1)} %iota.36), dimensions={0}, to_apply=%region_2.3 | sort | flops 2048 | bytes 4096 | tf_op jit(solution)/shard_map/jit(argsort)/sort | solution.py:45
  5.3 1.9 gather_fusion
  7.9 7.3 %all-to-all-start = ((s32[32,1,8]{2,1,0:T(1,128)}), s32[32,1,8]{2,1,0:T(1,128)S(1)}, u32[]{:S(2)}, u32[]{:S(2)}) async-start(s32[32,1,8]{2,1,0:T(1,128)} %bitcast), calls=%async_computation | async-start | bytes 32768 | tf_op jit(solution)/shard_map/all_to_all | solution.py:48
  15.2 1.5 reshape.152
  17.1 5.2 %all-to-all-done = s32[32,1,8]{2,1,0:T(1,128)S(1)} async-done(((s32[32,1,8]{2,1,0:T(1,128)}), s32[32,1,8]{2,1,0:T(1,128)S(1)}, u32[]{:S(2)}, u32[]{:S(2)}) %all-to-all-start) | async-done | bytes 1056 | tf_op jit(solution)/shard_map/all_to_all | solution.py:48
  22.3 1.6 fusion.18
  23.9 2.6 %all-to-all-start.1 = ((f32[32,8,1024]{2,1,0:T(8,128)}), f32[32,8,1024]{2,1,0:T(8,128)S(1)}, u32[]{:S(2)}, u32[]{:S(2)}) async-start(f32[32,8,1024]{2,1,0:T(8,128)} %fusion.18), calls=%async_computation.1 | async-start | bytes 2097152 | tf_op jit(solution)/shard_map/all_to_all | solution.py:58
  26.6 3.2 %sort.32 = (s32[256]{0:T(256)}, s32[256]{0:T(256)S(1)}) sort(s32[256]{0:T(256)S(1)} %get-tuple-element.5, s32[256]{0:T(256)S(1)} %iota.37), dimensions={0}, to_apply=%region_3.4 | sort | flops 2048 | bytes 4096 | tf_op jit(solution)/shard_map/jit(argsort)/sort | solution.py:46
  30.6 22.2 %all-to-all-done.1 = f32[32,8,1024]{2,1,0:T(8,128)S(1)} async-done(((f32[32,8,1024]{2,1,0:T(8,128)}), f32[32,8,1024]{2,1,0:T(8,128)S(1)}, u32[]{:S(2)}, u32[]{:S(2)}) %all-to-all-start.1) | async-done | bytes 1048608 | tf_op jit(solution)/shard_map/all_to_all | solution.py:58
  54.2 1.3 copy.34
  55.5 4.2 %fusion.12 = f32[256,16,128]{2,1,0:T(8,128)S(1)} fusion(f32[256,16,64]{2,1,0:T(8,128)S(1)} %copy.34, s32[256,128]{1,0:T(8,128)S(1)} %eq.84, f32[256,128]{1,0:T(8,128)S(1)} %mul.64), kind=kOutput, calls=%fused_computation.21 | convolution fusion | flops 405274624 | bytes 3407872 | tf_op jit(solution)/shard_map/bpx,bsx->bps/dot_general | solution.py:66
  59.8 2.0 copy.53
  61.8 1.7 reshape.157
  63.6 1.3 collective-permute-start
  65.0 1.5 collective-permute-start.1
  66.5 3.8 %fusion.11 = f32[32,256,128,1]{2,0,1,3:T(8,128)S(1)} fusion(s32[256,128]{1,0:T(8,128)S(1)} %add_abs_fusion, f32[32,64]{1,0:T(8,128)S(1)} %copy-done.8, f32[32,1]{1,0:T(8,128)S(1)} %copy-done.7), kind=kOutput, calls=%fused_computation.16 | convolution fusion | flops 820021248 | bytes 4333696 | tf_op jit(solution)/shard_map/usk,dk->dus/dot_general | solution.py:93
  72.0 1.2 copy.36
  74.9 7.9 %fusion.4 = f32[32,128,16,8]{1,2,3,0:T(8,128)S(1)} fusion(f32[16,32,8,128]{3,0,2,1:T(8,128)S(1)} %copy.37, f32[16,32,8,128]{3,0,2,1:T(8,128)S(1)} %copy.36, f32[32,256,128,1]{2,0,1,3:T(8,128)S(1)} %fusion.11), kind=kOutput, calls=%fused_computation.9 | convolution fusion | flops 1611661312 | bytes 10485760 | tf_op jit(solution)/shard_map/pdju,dus->pdjs/dot_general | solution.py:94
  83.1 6.6 %fusion.1 = f32[256,16,64]{2,1,0:T(8,128)S(1)} fusion(f32[256,16,128]{2,1,0:T(8,128)S(1)} %bitcast_multiply_fusion, s32[256,128]{1,0:T(8,128)S(1)} %eq.84), kind=kOutput, calls=%fused_computation.6 | convolution fusion | flops 404750336 | bytes 3276800 | tf_op jit(solution)/shard_map/bps,bsx->bpx/dot_general | solution.py:98
  91.1 2.2 %gather_fusion.2 = f32[256,1024]{1,0:T(8,128)} fusion(f32[256,1024]{1,0:T(8,128)S(1)} %copy.40, s32[1024]{0:T(1024)} %copy-done.9), kind=kCustom, calls=%fused_computation.2 | custom fusion | bytes 2098176 | tf_op jit(solution)/shard_map/gather | solution.py:101
  93.3 7.7 %all-to-all-start.2 = ((f32[32,8,1024]{2,1,0:T(8,128)}), f32[32,8,1024]{2,1,0:T(8,128)S(1)}, u32[]{:S(2)}, u32[]{:S(2)}) async-start(f32[32,8,1024]{2,1,0:T(8,128)} %bitcast.17), calls=%async_computation.2 | async-start | bytes 2097152 | tf_op jit(solution)/shard_map/all_to_all | solution.py:102
  102.2 24.9 %all-to-all-done.2 = f32[32,8,1024]{2,1,0:T(8,128)S(1)} async-done(((f32[32,8,1024]{2,1,0:T(8,128)}), f32[32,8,1024]{2,1,0:T(8,128)S(1)}, u32[]{:S(2)}, u32[]{:S(2)}) %all-to-all-start.2) | async-done | bytes 1048608 | tf_op jit(solution)/shard_map/all_to_all | solution.py:102
  129.2 38.5 %all-reduce = (f32[16]{0:T(128)S(1)}, f32[16]{0:T(128)S(1)}) all-reduce(f32[16]{0:T(128)S(1)} %get-tuple-element.17, f32[16]{0:T(128)S(1)} %get-tuple-element.18), channel_id=1, replica_groups=mesh['det'=4,'tm'=8] {'det','tm'}, use_global_device_ids=true, to_apply=%region_1.0 | all-reduce | flops 32 | bytes 256 | tf_op jit(solution)/shard_map/psum | solution.py:42
  168.0 40.8 %psum.23 = f32[16]{0:T(128)S(1)} all-reduce(f32[16]{0:T(128)S(1)} %get-tuple-element.9), channel_id=1, replica_groups=mesh['det'=4,'tm'=8] {'det','tm'}, use_global_device_ids=true, to_apply=%region_7.8 | all-reduce | flops 16 | bytes 128 | tf_op jit(solution)/shard_map/psum | solution.py:118
  (62 shorter events, 14.5 us)
Async XLA Ops:
  4.7 0.6 copy-start.9
  7.9 14.4 %all-to-all-start = ((s32[32,1,8]{2,1,0:T(1,128)}), s32[32,1,8]{2,1,0:T(1,128)S(1)}, u32[]{:S(2)}, u32[]{:S(2)}) async-start(s32[32,1,8]{2,1,0:T(1,128)} %bitcast), calls=%async_computation | async-start | bytes 32768 | tf_op jit(solution)/shard_map/all_to_all | solution.py:48
  17.0 12.7 %copy-start.10 = (f32[32]{0:T(128)S(1)}, f32[32]{0:T(128)}, u32[]{:S(2)}) copy-start(f32[32]{0:T(128)} %param.16) | copy-start | bytes 388
  17.0 13.4 %copy-start.5 = (s32[32,1024]{1,0:T(8,128)S(1)}, s32[32,1024]{1,0:T(8,128)}, u32[]{:S(2)}) copy-start(s32[32,1024]{1,0:T(8,128)} %param.14) | copy-start | bytes 393220
  17.1 13.4 %copy-start.6 = (f32[32,1024]{1,0:T(8,128)S(1)}, f32[32,1024]{1,0:T(8,128)}, u32[]{:S(2)}) copy-start(f32[32,1024]{1,0:T(8,128)} %param.15) | copy-start | bytes 393220
  23.9 28.9 %all-to-all-start.1 = ((f32[32,8,1024]{2,1,0:T(8,128)}), f32[32,8,1024]{2,1,0:T(8,128)S(1)}, u32[]{:S(2)}, u32[]{:S(2)}) async-start(f32[32,8,1024]{2,1,0:T(8,128)} %fusion.18), calls=%async_computation.1 | async-start | bytes 2097152 | tf_op jit(solution)/shard_map/all_to_all | solution.py:58
  61.8 4.7 %copy-start.7 = (f32[32,1]{1,0:T(8,128)S(1)}, f32[32,1]{1,0:T(8,128)}, u32[]{:S(2)}) copy-start(f32[32,1]{1,0:T(8,128)} %copy.30) | copy-start | bytes 388
  61.8 4.7 %copy-start.8 = (f32[32,64]{1,0:T(8,128)S(1)}, f32[32,64]{1,0:T(8,128)}, u32[]{:S(2)}) copy-start(f32[32,64]{1,0:T(8,128)} %param.17) | copy-start | bytes 24580
  63.6 6.7 %collective-permute-start = (f32[16,32,64]{2,1,0:T(8,128)S(1)}, f32[16,32,64]{2,1,0:T(8,128)S(1)}, u32[]{:S(2)}, u32[]{:S(2)}) collective-permute-start(f32[16,32,64]{2,1,0:T(8,128)S(1)} %get-tuple-element.13), channel_id=1, source_target_pairs={{0,1},{1,2},{2,3},{3,4},{4,5},{5,6},{6,7},{8,9},{9,10},{10,11},{11... | collective-permute-start | bytes 393224 | tf_op jit(solution)/shard_map/ppermute | solution.py:17
  65.0 5.3 %collective-permute-start.1 = (f32[16,32,64]{2,1,0:T(8,128)S(1)}, f32[16,32,64]{2,1,0:T(8,128)S(1)}, u32[]{:S(2)}, u32[]{:S(2)}) collective-permute-start(f32[16,32,64]{2,1,0:T(8,128)S(1)} %get-tuple-element.14), channel_id=1, source_target_pairs={{1,0},{2,1},{3,2},{4,3},{5,4},{6,5},{7,6},{9,8},{10,9},{11,10},{12... | collective-permute-start | bytes 393224 | tf_op jit(solution)/shard_map/ppermute | solution.py:19
  93.3 33.9 %all-to-all-start.2 = ((f32[32,8,1024]{2,1,0:T(8,128)}), f32[32,8,1024]{2,1,0:T(8,128)S(1)}, u32[]{:S(2)}, u32[]{:S(2)}) async-start(f32[32,8,1024]{2,1,0:T(8,128)} %bitcast.17), calls=%async_computation.2 | async-start | bytes 2097152 | tf_op jit(solution)/shard_map/all_to_all | solution.py:102
  127.5 1.4 copy-start
  127.5 1.4 copy-start.2
  127.5 1.4 copy-start.4
  128.6 80.2 %copy-start.3 = (f32[16,8192]{1,0:T(8,128)S(1)}, f32[16,8192]{1,0:T(8,128)}, u32[]{:S(2)}) copy-start(f32[16,8192]{1,0:T(8,128)} %param.9) | copy-start | bytes 1572868
  168.0 41.9 %copy-start.1 = (f32[16,8192]{1,0:T(8,128)}, f32[16,8192]{1,0:T(8,128)S(1)}, u32[]{:S(2)}) copy-start(f32[16,8192]{1,0:T(8,128)S(1)} %get-tuple-element.10) | copy-start | bytes 1572868
where the time goes:
time: 211 us; the launch traced here: 210 us
  blocking collectives  79.3 us (38%)
  waiting for transfers between devices  52.4 us (25%)
  matrix products  24.9 us (12%)
  local copies, waits for them, and re-layouts  21.1 us (10%)
  starting transfers between devices  20.4 us (10%)
  other arithmetic  10.8 us (5%)
    psum x1, blocking collectives, per_device(): norm_new = lax.psum(jnp.sum(new_residual * scaled, axis=1), ('det', 'tm'))  40.8 us
    psum x1, blocking collectives, per_device(): norm_old = lax.psum(local_old, ('det', 'tm'))  38.5 us
    all_to_all x1, waiting for transfers between devices, per_device(): lax.all_to_all(partial_value, ('det', 'tm'), split_axis=0, concat_axis=0,...  24.9 us
    all_to_all x1, waiting for transfers between devices, per_device(): lax.all_to_all(served, ('det', 'tm'), split_axis=0, concat_axis=0, tiled=...  22.2 us
    dot_general x1, matrix products, per_device(): jnp.einsum('pdju,dus->pdjs', windows, toeplitz, precision=lax.Precision.H...  7.91 us
    all_to_all x1, starting transfers between devices, per_device(): lax.all_to_all(partial_value, ('det', 'tm'), split_axis=0, concat_axis=0,...  7.69 us
    all_to_all x1, starting transfers between devices, per_device(): lax.all_to_all(requests, ('det', 'tm'), split_axis=0, concat_axis=0, tile...  7.3 us
    dot_general x1, matrix products, per_device(): jnp.einsum('bps,bsx->bpx', weighted, pixel_hot, precision=lax.Precision.H...  6.59 us
  transfers between devices with their start and end apart: 5, of which 3 were waited for; matrix products, arithmetic and copies ran while one was open for 5% of the time, Pallas kernels for 0%

commit v1 on v0

--- a/solution.py
+++ b/solution.py
@@ -1,6 +1,10 @@
+import functools
+
 import jax
 import jax.numpy as jnp
 from jax import lax
+from jax.experimental import pallas as pl
+from jax.experimental.pallas import tpu as pltpu
 from jax.sharding import PartitionSpec as P
 
 PX = 64
@@ -23,6 +27,60 @@
     return cells
 
 
+def share_kernel(spans, devices, part_ref, out_ref, held, send_sem, recv_sem):
+    me = lax.axis_index("det") * spans + lax.axis_index("tm")
+    barrier = pltpu.get_barrier_semaphore()
+
+    def place(step):
+        peer = lax.rem(me + step, devices)
+        return (peer // spans, lax.rem(peer, spans))
+
+    def copy_to(step):
+        return pltpu.make_async_remote_copy(
+            src_ref=part_ref,
+            dst_ref=held.at[step],
+            send_sem=send_sem.at[step],
+            recv_sem=recv_sem.at[step],
+            device_id=place(step),
+            device_id_type=pl.DeviceIdType.MESH,
+        )
+
+    @pl.loop(1, devices)
+    def _(step):
+        pl.semaphore_signal(
+            barrier, inc=1, device_id=place(step), device_id_type=pl.DeviceIdType.MESH
+        )
+
+    pl.semaphore_wait(barrier, devices - 1)
+
+    @pl.loop(1, devices)
+    def _(step):
+        copy_to(step).start()
+
+    held[0] = part_ref[...]
+
+    @pl.loop(1, devices)
+    def _(step):
+        copy_to(step).wait()
+
+    out_ref[...] = jnp.sum(held[...], axis=0)
+
+
+def sum_everywhere(part, spans, devices):
+    return pl.pallas_call(
+        functools.partial(share_kernel, spans, devices),
+        out_shape=jax.ShapeDtypeStruct(part.shape, jnp.float32),
+        in_specs=[pl.BlockSpec(memory_space=pltpu.VMEM)],
+        out_specs=pl.BlockSpec(memory_space=pltpu.VMEM),
+        scratch_shapes=[
+            pltpu.VMEM((devices,) + part.shape, jnp.float32),
+            pltpu.SemaphoreType.DMA((devices,)),
+            pltpu.SemaphoreType.DMA((devices,)),
+        ],
+        compiler_params=pltpu.CompilerParams(collective_id=0, has_side_effects=True),
+    )(part)
+
+
 def per_device(
     iterate, residual, direction, precond, patch_ids, pixel_in, weights, filter_diag, filter_band
 ):
@@ -38,8 +96,6 @@
     per_owner = blocks // devices
     own_patches = iterate.shape[1] // PX
     width = probes * PX
-    local_old = jnp.sum(residual * precond * residual, axis=1)
-    norm_old = lax.psum(local_old, ("det", "tm"))
     patch_flat = patch_ids.reshape(blocks)
     owners = patch_flat // own_patches
     sort_order = jnp.argsort(owners, stable=True)
@@ -109,13 +165,24 @@
     image_map = (
         summed.reshape(own_patches, probes, PX).transpose(1, 0, 2).reshape(probes, own_patches * PX)
     )
-    local_curv = jnp.sum(direction * image_map, axis=1)
-    curvature = lax.psum(local_curv, ("det", "tm"))
+    lean = precond * residual
+    drop = precond * image_map
+    sums = jnp.stack(
+        [
+            jnp.sum(residual * lean, axis=1),
+            jnp.sum(direction * image_map, axis=1),
+            jnp.sum(image_map * lean, axis=1),
+            jnp.sum(image_map * drop, axis=1),
+        ]
+    )
+    part = jnp.pad(sums, ((0, 4), (0, 128 - probes)))
+    total = sum_everywhere(part, spans, devices)
+    norm_old, curvature, cross, square = (total[i, :probes] for i in range(4))
     step_size = norm_old / curvature
+    norm_new = norm_old - step_size * (2.0 * cross - step_size * square)
     new_iterate = iterate + step_size[:, None] * direction
     new_residual = residual - step_size[:, None] * image_map
     scaled = precond * new_residual
-    norm_new = lax.psum(jnp.sum(new_residual * scaled, axis=1), ("det", "tm"))
     new_direction = scaled + (norm_new / norm_old)[:, None] * direction
     return (new_iterate, new_residual, new_direction)
 

time: 211 us -> 142 us (0.67)
  blocking collectives: 79.3 us -> 0 us
  Pallas kernels: 0 us -> 9.65 us
    psum x2 -> x0, blocking collectives: 79.3 us -> none  [the longest x1 40.8 us: per_device(): norm_new = lax.psum(jnp.sum(new_residual * scaled, axis=1), ('det', 'tm'))]
    pallas_call x0 -> x1, Pallas kernels: none -> 9.65 us  [sum_everywhere(): pl.pallas_call(functools.partial(share_kernel, spans, devices), out_shape...]
  transfers between devices with their start and end apart: 5 -> 5, of which waited for: 3 -> 3; matrix products, arithmetic and copies ran while one was open for 5% -> 8% of each run, Pallas kernels for 0% -> 0%
where the time goes in v1:
time: 142 us
  waiting for transfers between devices  52 us (37%)
  matrix products  25.6 us (18%)
  local copies, waits for them, and re-layouts  21.3 us (15%)
  starting transfers between devices  20 us (14%)
  other arithmetic  12.3 us (9%)
  Pallas kernels  9.65 us (7%)
    all_to_all x1, waiting for transfers between devices, per_device(): lax.all_to_all(partial_value, ('det', 'tm'), split_axis=0, concat_axis=0,...  24.5 us
    all_to_all x1, waiting for transfers between devices, per_device(): lax.all_to_all(served, ('det', 'tm'), split_axis=0, concat_axis=0, tiled=...  22.2 us
    pallas_call x1, Pallas kernels, sum_everywhere(): pl.pallas_call(functools.partial(share_kernel, spans, devices), out_shape...  9.65 us
    dot_general x1, matrix products, per_device(): jnp.einsum('pdju,dus->pdjs', windows, toeplitz, precision=lax.Precision.H...  7.91 us
    all_to_all x1, starting transfers between devices, per_device(): lax.all_to_all(requests, ('det', 'tm'), split_axis=0, concat_axis=0, tile...  7.3 us
    all_to_all x1, starting transfers between devices, per_device(): lax.all_to_all(partial_value, ('det', 'tm'), split_axis=0, concat_axis=0,...  7.29 us
    dot_general x1, matrix products, per_device(): jnp.einsum('bps,bsx->bpx', weighted, pixel_hot, precision=lax.Precision.H...  6.59 us
    all_to_all x1, waiting for transfers between devices, per_device(): lax.all_to_all(requests, ('det', 'tm'), split_axis=0, concat_axis=0, tile...  5.26 us
  transfers between devices with their start and end apart: 5, of which 3 were waited for; matrix products, arithmetic and copies ran while one was open for 8% of the time, Pallas kernels for 0%

profile of v1, /device:TPU:0, one launch (start us, length us, event | category | flops | bytes accessed | tf_op | source)
XLA Modules:
  0.0 141.8 jit_solution(780248315480360364)
XLA Ops:
  1.5 3.2 %sort.31 = (s32[256]{0:T(256)}, s32[256]{0:T(256)S(1)}) sort(s32[256]{0:T(256)S(1)} %and_select_fusion, s32[256]{0:T(256)S(1)} %iota.36), dimensions={0}, to_apply=%region_1.2 | sort | flops 2048 | bytes 4096 | tf_op jit(solution)/shard_map/jit(argsort)/sort | solution.py:101
  5.3 1.9 %gather_fusion = s32[256]{0:T(256)S(1)} fusion(s32[256]{0:T(256)S(1)} %reshape.190, s32[1024]{0:T(1024)S(1)} %pad_clamp_fusion.1), kind=kCustom, calls=%fused_computation | custom fusion | bytes 3072 | tf_op jit(solution)/shard_map/gather | solution.py:103
  7.9 7.3 %all-to-all-start = ((s32[32,1,8]{2,1,0:T(1,128)}), s32[32,1,8]{2,1,0:T(1,128)S(1)}, u32[]{:S(2)}, u32[]{:S(2)}) async-start(s32[32,1,8]{2,1,0:T(1,128)} %bitcast.1), calls=%async_computation | async-start | bytes 32768 | tf_op jit(solution)/shard_map/all_to_all | solution.py:104
  15.2 1.5 %reshape.191 = f32[16,128,64]{2,1,0:T(8,128)S(1)} reshape(f32[16,8192]{1,0:T(8,128)} %param.11) | data formatting | bytes 1048576 | tf_op jit(solution)/shard_map/reshape | solution.py:109
  17.1 5.3 %all-to-all-done = s32[32,1,8]{2,1,0:T(1,128)S(1)} async-done(((s32[32,1,8]{2,1,0:T(1,128)}), s32[32,1,8]{2,1,0:T(1,128)S(1)}, u32[]{:S(2)}, u32[]{:S(2)}) %all-to-all-start) | async-done | bytes 1056 | tf_op jit(solution)/shard_map/all_to_all | solution.py:104
  22.3 1.6 %fusion.19 = f32[32,8,1024]{2,1,0:T(8,128)} fusion(f32[128,1024,1]{0,1,2:T(8,128)S(1)} %bitcast.85, s32[32,8]{1,0:T(8,128)S(1)} %bitcast.86), kind=kOutput, calls=%fused_computation.38 | convolution fusion | flops 402685952 | bytes 1573888 | tf_op jit(solution)/shard_map/dot_general | solution.py:111
  23.9 2.6 %all-to-all-start.1 = ((f32[32,8,1024]{2,1,0:T(8,128)}), f32[32,8,1024]{2,1,0:T(8,128)S(1)}, u32[]{:S(2)}, u32[]{:S(2)}) async-start(f32[32,8,1024]{2,1,0:T(8,128)} %fusion.19), calls=%async_computation.1 | async-start | bytes 2097152 | tf_op jit(solution)/shard_map/all_to_all | solution.py:114
  26.6 3.2 %sort.32 = (s32[256]{0:T(256)}, s32[256]{0:T(256)S(1)}) sort(s32[256]{0:T(256)S(1)} %get-tuple-element.5, s32[256]{0:T(256)S(1)} %iota.37), dimensions={0}, to_apply=%region_2.3 | sort | flops 2048 | bytes 4096 | tf_op jit(solution)/shard_map/jit(argsort)/sort | solution.py:102
  30.6 22.2 %all-to-all-done.1 = f32[32,8,1024]{2,1,0:T(8,128)S(1)} async-done(((f32[32,8,1024]{2,1,0:T(8,128)}), f32[32,8,1024]{2,1,0:T(8,128)S(1)}, u32[]{:S(2)}, u32[]{:S(2)}) %all-to-all-start.1) | async-done | bytes 1048608 | tf_op jit(solution)/shard_map/all_to_all | solution.py:114
  54.2 1.3 copy.35
  55.5 4.2 %fusion.12 = f32[256,16,128]{2,1,0:T(8,128)S(1)} fusion(f32[256,16,64]{2,1,0:T(8,128)S(1)} %copy.35, s32[256,128]{1,0:T(8,128)S(1)} %eq.84, f32[256,128]{1,0:T(8,128)S(1)} %mul.103), kind=kOutput, calls=%fused_computation.21 | convolution fusion | flops 405274624 | bytes 3407872 | tf_op jit(solution)/shard_map/bpx,bsx->bps/dot_general | solution.py:122
  59.8 2.0 %copy.55 = f32[32,8,16,128]{3,1,0,2:T(8,128)} copy(f32[32,8,16,128]{3,2,1,0:T(8,128)S(1)} %bitcast.76) | data formatting | bytes 4194304 | tf_op jit(solution)/shard_map/reshape | solution.py:126
  61.8 1.7 %reshape.196 = f32[16,32,1024]{2,1,0:T(8,128)S(1)} reshape(f32[16,32,8,128]{3,2,1,0:T(8,128)} %bitcast.77) | data formatting | bytes 4194304 | tf_op jit(solution)/shard_map/reshape | solution.py:128
  63.6 1.3 collective-permute-start
  64.9 1.5 %collective-permute-start.1 = (f32[16,32,64]{2,1,0:T(8,128)S(1)}, f32[16,32,64]{2,1,0:T(8,128)S(1)}, u32[]{:S(2)}, u32[]{:S(2)}) collective-permute-start(f32[16,32,64]{2,1,0:T(8,128)S(1)} %get-tuple-element.17), channel_id=1, source_target_pairs={{1,0},{2,1},{3,2},{4,3},{5,4},{6,5},{7,6},{9,8},{10,9},{11,10},{12... | collective-permute-start | bytes 393224 | tf_op jit(solution)/shard_map/ppermute | solution.py:23
  66.4 4.5 %fusion.11 = f32[32,256,128,1]{2,0,1,3:T(8,128)S(1)} fusion(s32[256,128]{1,0:T(8,128)S(1)} %add_abs_fusion, f32[32,64]{1,0:T(8,128)} %param.17, f32[32,1]{1,0:T(8,128)} %copy.31), kind=kOutput, calls=%fused_computation.16 | convolution fusion | flops 820021248 | bytes 4333696 | tf_op jit(solution)/shard_map/usk,dk->dus/dot_general | solution.py:149
  72.6 1.2 copy.37
  75.6 7.9 %fusion.4 = f32[32,128,16,8]{1,2,3,0:T(8,128)S(1)} fusion(f32[16,32,8,128]{3,0,2,1:T(8,128)S(1)} %copy.38, f32[16,32,8,128]{3,0,2,1:T(8,128)S(1)} %copy.37, f32[32,256,128,1]{2,0,1,3:T(8,128)S(1)} %fusion.11), kind=kOutput, calls=%fused_computation.9 | convolution fusion | flops 1611661312 | bytes 10485760 | tf_op jit(solution)/shard_map/pdju,dus->pdjs/dot_general | solution.py:150
  83.7 6.6 %fusion.1 = f32[256,16,64]{2,1,0:T(8,128)S(1)} fusion(f32[256,16,128]{2,1,0:T(8,128)S(1)} %bitcast_multiply_fusion, s32[256,128]{1,0:T(8,128)S(1)} %eq.84), kind=kOutput, calls=%fused_computation.6 | convolution fusion | flops 404750336 | bytes 3276800 | tf_op jit(solution)/shard_map/bps,bsx->bpx/dot_general | solution.py:154
  91.7 2.2 %gather_fusion.2 = f32[256,1024]{1,0:T(8,128)} fusion(f32[256,1024]{1,0:T(8,128)S(1)} %copy.41, s32[1024]{0:T(1024)} %copy-done.6), kind=kCustom, calls=%fused_computation.2 | custom fusion | bytes 2098176 | tf_op jit(solution)/shard_map/gather | solution.py:157
  93.9 7.3 %all-to-all-start.2 = ((f32[32,8,1024]{2,1,0:T(8,128)}), f32[32,8,1024]{2,1,0:T(8,128)S(1)}, u32[]{:S(2)}, u32[]{:S(2)}) async-start(f32[32,8,1024]{2,1,0:T(8,128)} %bitcast.18), calls=%async_computation.2 | async-start | bytes 2097152 | tf_op jit(solution)/shard_map/all_to_all | solution.py:158
  102.7 24.5 %all-to-all-done.2 = f32[32,8,1024]{2,1,0:T(8,128)S(1)} async-done(((f32[32,8,1024]{2,1,0:T(8,128)}), f32[32,8,1024]{2,1,0:T(8,128)S(1)}, u32[]{:S(2)}, u32[]{:S(2)}) %all-to-all-start.2) | async-done | bytes 1048608 | tf_op jit(solution)/shard_map/all_to_all | solution.py:158
  129.9 9.7 %shard_map.112 = f32[8,128]{1,0:T(8,128)} custom-call(f32[8,128]{1,0:T(8,128)} %select_maximum_fusion.part_ref), custom_call_target="tpu_custom_call" | custom-call | tf_op jit(solution)/shard_map/pallas_call | solution.py:70
  140.5 1.3 multiply_add_fusion
  (56 shorter events, 14.9 us)
Async XLA Ops:
  4.7 0.6 copy-start.6
  7.9 14.4 %all-to-all-start = ((s32[32,1,8]{2,1,0:T(1,128)}), s32[32,1,8]{2,1,0:T(1,128)S(1)}, u32[]{:S(2)}, u32[]{:S(2)}) async-start(s32[32,1,8]{2,1,0:T(1,128)} %bitcast.1), calls=%async_computation | async-start | bytes 32768 | tf_op jit(solution)/shard_map/all_to_all | solution.py:104
  17.0 12.7 %copy-start.4 = (s32[32,1024]{1,0:T(8,128)S(1)}, s32[32,1024]{1,0:T(8,128)}, u32[]{:S(2)}) copy-start(s32[32,1024]{1,0:T(8,128)} %param.14) | copy-start | bytes 393220
  17.0 12.7 %copy-start.5 = (f32[32,1024]{1,0:T(8,128)S(1)}, f32[32,1024]{1,0:T(8,128)}, u32[]{:S(2)}) copy-start(f32[32,1024]{1,0:T(8,128)} %param.15) | copy-start | bytes 393220
  22.3 7.5 %copy-start.7 = (f32[32]{0:T(128)S(1)}, f32[32]{0:T(128)}, u32[]{:S(2)}) copy-start(f32[32]{0:T(128)} %param.16) | copy-start | bytes 388
  23.9 28.9 %all-to-all-start.1 = ((f32[32,8,1024]{2,1,0:T(8,128)}), f32[32,8,1024]{2,1,0:T(8,128)S(1)}, u32[]{:S(2)}, u32[]{:S(2)}) async-start(f32[32,8,1024]{2,1,0:T(8,128)} %fusion.19), calls=%async_computation.1 | async-start | bytes 2097152 | tf_op jit(solution)/shard_map/all_to_all | solution.py:114
  63.6 7.3 %collective-permute-start = (f32[16,32,64]{2,1,0:T(8,128)S(1)}, f32[16,32,64]{2,1,0:T(8,128)S(1)}, u32[]{:S(2)}, u32[]{:S(2)}) collective-permute-start(f32[16,32,64]{2,1,0:T(8,128)S(1)} %get-tuple-element.16), channel_id=1, source_target_pairs={{0,1},{1,2},{2,3},{3,4},{4,5},{5,6},{6,7},{8,9},{9,10},{10,11},{11... | collective-permute-start | bytes 393224 | tf_op jit(solution)/shard_map/ppermute | solution.py:21
  64.9 6.0 %collective-permute-start.1 = (f32[16,32,64]{2,1,0:T(8,128)S(1)}, f32[16,32,64]{2,1,0:T(8,128)S(1)}, u32[]{:S(2)}, u32[]{:S(2)}) collective-permute-start(f32[16,32,64]{2,1,0:T(8,128)S(1)} %get-tuple-element.17), channel_id=1, source_target_pairs={{1,0},{2,1},{3,2},{4,3},{5,4},{6,5},{7,6},{9,8},{10,9},{11,10},{12... | collective-permute-start | bytes 393224 | tf_op jit(solution)/shard_map/ppermute | solution.py:23
  93.9 7.3 %copy-start.3 = (f32[8192]{0:T(1024)S(1)}, f32[8192]{0:T(1024)}, u32[]{:S(2)}) copy-start(f32[8192]{0:T(1024)} %param.12) | copy-start | bytes 98308
  93.9 33.3 %all-to-all-start.2 = ((f32[32,8,1024]{2,1,0:T(8,128)}), f32[32,8,1024]{2,1,0:T(8,128)S(1)}, u32[]{:S(2)}, u32[]{:S(2)}) async-start(f32[32,8,1024]{2,1,0:T(8,128)} %bitcast.18), calls=%async_computation.2 | async-start | bytes 2097152 | tf_op jit(solution)/shard_map/all_to_all | solution.py:158
  127.5 1.5 %copy-start = (f32[16,8192]{1,0:T(8,128)S(1)}, f32[16,8192]{1,0:T(8,128)}, u32[]{:S(2)}) copy-start(f32[16,8192]{1,0:T(8,128)} %param.11) | copy-start | bytes 1572868
  127.5 1.5 %copy-start.1 = (f32[16,8192]{1,0:T(8,128)S(1)}, f32[16,8192]{1,0:T(8,128)}, u32[]{:S(2)}) copy-start(f32[16,8192]{1,0:T(8,128)} %param.10) | copy-start | bytes 1572868
  128.3 12.2 %copy-start.2 = (f32[16,8192]{1,0:T(8,128)S(1)}, f32[16,8192]{1,0:T(8,128)}, u32[]{:S(2)}) copy-start(f32[16,8192]{1,0:T(8,128)} %param.9) | copy-start | bytes 1572868

commit v2 on v1

v2 whole, which is shorter than its diff:
```python
import functools

import jax
import jax.numpy as jnp
from jax import lax
from jax.experimental import pallas as pl
from jax.experimental.pallas import tpu as pltpu
from jax.sharding import PartitionSpec as P

PX = 64


def halves(values):
    top = values.astype(jnp.bfloat16)
    return top, (values - top.astype(jnp.float32)).astype(jnp.bfloat16)


def vmem(count):
    return [pl.BlockSpec(memory_space=pltpu.VMEM)] * count


def smem():
    return pl.BlockSpec(memory_space=pltpu.SMEM)


def serve_kernel(asked_ref, table_ref, out_ref):
    @pl.loop(0, out_ref.shape[0], step=8)
    def _(first):
        for i in range(8):
            out_ref[first + i] = table_ref[asked_ref[first + i]]


def serve(asked, table):
    return pl.pallas_call(
        serve_kernel,
        out_shape=jax.ShapeDtypeStruct(asked.shape + table.shape[1:], jnp.float32),
        in_specs=[smem()] + vmem(1),
        out_specs=vmem(1)[0],
    )(asked, table)


def gather_up_kernel(asked_ref, parts_ref, out_ref):
    out_ref[...] = jnp.zeros_like(out_ref)

    @pl.loop(0, parts_ref.shape[0], step=8)
    def _(first):
        for i in range(8):
            row = asked_ref[first + i]
            out_ref[row] = out_ref[row] + parts_ref[first + i]


def gather_up(asked, parts, rows):
    return pl.pallas_call(
        gather_up_kernel,
        out_shape=jax.ShapeDtypeStruct((rows,) + parts.shape[1:], jnp.float32),
        in_specs=[smem()] + vmem(1),
        out_specs=vmem(1)[0],
    )(asked, parts)


def scan_kernel(slot_ref, patches_ref, pixel_ref, gain_ref, line_ref, head_ref, tail_ref):
    rows, blocks, _ = pixel_ref.shape
    half = rows // 2
    left = lax.broadcasted_iota(jnp.int32, (16, 128), 1) < 64

    def one_row(d):
        pixels, gains = pixel_ref[d], gain_ref[d]
        for j in range(blocks):
            pixel = jnp.broadcast_to(pixels[j : j + 1], (8, 128))
            gain = jnp.broadcast_to(gains[j : j + 1], (8, 128))
            patch = patches_ref[slot_ref[d * blocks + j]]
            line_ref[d, 16 * j : 16 * j + 8] = (
                jnp.take_along_axis(patch, pixel, axis=1) * gain
            )
            line_ref[d, 16 * j + 8 : 16 * j + 16] = (
                jnp.take_along_axis(patch, pixel + 64, axis=1) * gain
            )

    @pl.loop(0, half)
    def _(d):
        one_row(d)
        one_row(d + half)
        last = 16 * (blocks - 1)
        head_ref[d] = jnp.where(
            left, line_ref[d, 0:16], pltpu.roll(line_ref[d + half, 0:16], 64, 1)
        )
        tail_ref[d] = jnp.where(
            left,
            pltpu.roll(line_ref[d + half, last : last + 16], 64, 1),
            line_ref[d, last : last + 16],
        )


def scan(slot, patches, pixel, gain):
    rows, blocks, _ = pixel.shape
    edge = jax.ShapeDtypeStruct((rows // 2, 16, 128), jnp.float32)
    return pl.pallas_call(
        scan_kernel,
        out_shape=(jax.ShapeDtypeStruct((rows, 16 * blocks, 128), jnp.float32), edge, edge),
        in_specs=[smem()] + vmem(3),
        out_specs=tuple(vmem(3)),
    )(slot, patches, pixel, gain)


def project_kernel(
    slot_ref, line_ref, before_ref, after_ref, base_ref, pixel_ref, gain_ref, out_ref
):
    rows, blocks, _ = pixel_ref.shape
    half = rows // 2
    down = lax.broadcasted_iota(jnp.int32, (128, 128), 0)
    across = lax.broadcasted_iota(jnp.int32, (128, 128), 1)
    place = lax.broadcasted_iota(jnp.int32, (64, 128), 0)

    def one_row(d, before, after):
        base = jnp.broadcast_to(base_ref[d], (128, 256))
        turned = pltpu.roll(base, 0, 1, stride=1, stride_axis=0)
        near, far = turned[:, :128], turned[:, 128:]
        band = jnp.concatenate(
            [jnp.where(down > across, far, 0.0), near, jnp.where(down < across, far, 0.0)], axis=0
        )
        band_top, band_low = halves(band)
        cells = jnp.concatenate([before, line_ref[d], after], axis=0)
        top, low = halves(cells)
        wide_top = jnp.concatenate(
            [top[16 * o : 16 * (o + blocks)] for o in range(3)], axis=1
        )
        wide_low = jnp.concatenate(
            [low[16 * o : 16 * (o + blocks)] for o in range(3)], axis=1
        )
        filtered = (
            jnp.dot(wide_top, band_top, preferred_element_type=jnp.float32)
            + jnp.dot(wide_low, band_top, preferred_element_type=jnp.float32)
            + jnp.dot(wide_top, band_low, preferred_element_type=jnp.float32)
        )
        pixels, gains = pixel_ref[d], gain_ref[d]
        for j in range(blocks):
            gain = jnp.broadcast_to(gains[j : j + 1], (16, 128))
            pixel = jnp.broadcast_to(pixels[j : j + 1], (64, 128))
            hot = jnp.where(place == pixel, 1.0, 0.0).astype(jnp.bfloat16)
            both = jnp.concatenate(halves(filtered[16 * j : 16 * j + 16] * gain), axis=0)
            added = lax.dot_general(
                both, hot, (((1,), (1,)), ((), ())), preferred_element_type=jnp.float32
            )
            added = added[:16] + added[16:]
            out_ref[slot_ref[d * blocks + j]] = jnp.concatenate([added[:8], added[8:]], axis=1)

    @pl.loop(0, half)
    def _(d):
        before, after = before_ref[d], after_ref[d]
        one_row(d, before, after)
        one_row(d + half, pltpu.roll(before, 64, 1), pltpu.roll(after, 64, 1))


def project(slot, line, before, after, base, pixel, gain):
    rows, blocks, _ = pixel.shape
    return pl.pallas_call(
        project_kernel,
        out_shape=jax.ShapeDtypeStruct((rows * blocks, 8, 128), jnp.float32),
        in_specs=[smem()] + vmem(6),
        out_specs=vmem(1)[0],
        compiler_params=pltpu.CompilerParams(vmem_limit_bytes=40 * 1024 * 1024),
    )(slot, line, before, after, base, pixel, gain)


def share_kernel(spans, devices, part_ref, out_ref, held, send_sem, recv_sem):
    me = lax.axis_index("det") * spans + lax.axis_index("tm")
    barrier = pltpu.get_barrier_semaphore()

    def place(step):
        peer = lax.rem(me + step, devices)
        return (peer // spans, lax.rem(peer, spans))

    def copy_to(step):
        return pltpu.make_async_remote_copy(
            src_ref=part_ref,
            dst_ref=held.at[step],
            send_sem=send_sem.at[step],
            recv_sem=recv_sem.at[step],
            device_id=place(step),
            device_id_type=pl.DeviceIdType.MESH,
        )

    @pl.loop(1, devices)
    def _(step):
        pl.semaphore_signal(
            barrier, inc=1, device_id=place(step), device_id_type=pl.DeviceIdType.MESH
        )

    pl.semaphore_wait(barrier, devices - 1)

    @pl.loop(1, devices)
    def _(step):
        copy_to(step).start()

    held[0] = part_ref[...]

    @pl.loop(1, devices)
    def _(step):
        copy_to(step).wait()

    out_ref[...] = jnp.sum(held[...], axis=0)


def sum_everywhere(part, spans, devices):
    return pl.pallas_call(
        functools.partial(share_kernel, spans, devices),
        out_shape=jax.ShapeDtypeStruct(part.shape, jnp.float32),
        in_specs=[pl.BlockSpec(memory_space=pltpu.VMEM)],
        out_specs=pl.BlockSpec(memory_space=pltpu.VMEM),
        scratch_shapes=[
            pltpu.VMEM((devices,) + part.shape, jnp.float32),
            pltpu.SemaphoreType.DMA((devices,)),
            pltpu.SemaphoreType.DMA((devices,)),
        ],
        compiler_params=pltpu.CompilerParams(collective_id=0, has_side_effects=True),
    )(part)


def per_device(
    iterate, residual, direction, precond, patch_ids, pixel_in, weights, filter_diag, filter_band
):
    probes = iterate.shape[0]
    det_rows, time_blocks = patch_ids.shape
    half_band = filter_band.shape[1]
    groups = lax.axis_size("det")
    spans = lax.axis_size("tm")
    devices = groups * spans
    blocks = det_rows * time_blocks
    per_owner = blocks // devices
    own_patches = iterate.shape[1] // PX
    patch_flat = patch_ids.reshape(blocks)
    owners = patch_flat // own_patches
    numbers = jnp.arange(blocks, dtype=jnp.int32)
    earlier = (owners[:, None] == owners[None, :]) & (numbers[None, :] < numbers[:, None])
    slot = owners * per_owner + jnp.sum(earlier.astype(jnp.int32), axis=1)
    requests = jnp.sum(
        jnp.where(numbers[:, None] == slot[None, :], (patch_flat % own_patches)[None, :], 0), axis=1
    ).reshape(devices, per_owner)
    asked = lax.all_to_all(requests, ("det", "tm"), split_axis=0, concat_axis=0, tiled=True)
    asked = asked.reshape(blocks)
    table = (
        direction.reshape(2, 8, own_patches, PX).transpose(2, 1, 0, 3).reshape(own_patches, 8, 128)
    )
    served = serve(asked, table).reshape(devices, per_owner, 8, 128)
    fetched = lax.all_to_all(served, ("det", "tm"), split_axis=0, concat_axis=0, tiled=True)
    pixels = pixel_in.reshape(det_rows, time_blocks, 128)
    gains = weights.reshape(det_rows, time_blocks, 128)
    line, head, tail = scan(slot, fetched.reshape(blocks, 8, 128), pixels, gains)
    before = lax.ppermute(tail, "tm", [(i, i + 1) for i in range(spans - 1)])
    after = lax.ppermute(head, "tm", [(i + 1, i) for i in range(spans - 1)])
    base = jnp.concatenate(
        [
            filter_diag[:, None],
            filter_band,
            jnp.zeros((det_rows, 255 - 2 * half_band), jnp.float32),
            filter_band[:, ::-1],
        ],
        axis=1,
    )[:, None, :]
    parts = project(slot, line, before, after, base, pixels, gains)
    collected = lax.all_to_all(
        parts.reshape(devices, per_owner, 8, 128),
        ("det", "tm"),
        split_axis=0,
        concat_axis=0,
        tiled=True,
    ).reshape(blocks, 8, 128)
    image_map = (
        gather_up(asked, collected, own_patches)
        .reshape(own_patches, 8, 2, PX)
        .transpose(2, 1, 0, 3)
        .reshape(probes, own_patches * PX)
    )
    lean = precond * residual
    drop = precond * image_map
    sums = jnp.stack(
        [
            jnp.sum(residual * lean, axis=1),
            jnp.sum(direction * image_map, axis=1),
            jnp.sum(image_map * lean, axis=1),
            jnp.sum(image_map * drop, axis=1),
        ]
    )
    part = jnp.pad(sums, ((0, 4), (0, 128 - probes)))
    total = sum_everywhere(part, spans, devices)
    norm_old, curvature, cross, square = (total[i, :probes] for i in range(4))
    step_size = norm_old / curvature
    norm_new = norm_old - step_size * (2.0 * cross - step_size * square)
    new_iterate = iterate + step_size[:, None] * direction
    new_residual = residual - step_size[:, None] * image_map
    scaled = precond * new_residual
    new_direction = scaled + (norm_new / norm_old)[:, None] * direction
    return (new_iterate, new_residual, new_direction)


def solution(mesh):
    in_specs = (
        P(None, ("det", "tm")),
        P(None, ("det", "tm")),
        P(None, ("det", "tm")),
        P(("det", "tm")),
        P("det", "tm"),
        P("det", "tm"),
        P("det", "tm"),
        P("det"),
        P("det", None),
    )
    out_specs = (P(None, ("det", "tm")), P(None, ("det", "tm")), P(None, ("det", "tm")))
    return jax.shard_map(
        per_device, mesh=mesh, in_specs=in_specs, out_specs=out_specs, check_vma=False
    )
```

time: 142 us -> 134 us (0.944)
  Pallas kernels: 9.65 us -> 35.5 us
  matrix products: 25.6 us -> 0 us
  other arithmetic: 12.3 us -> 4.3 us
  waiting for transfers between devices: 52 us -> 58.7 us
  local copies, waits for them, and re-layouts: 21.3 us -> 14.8 us
    pallas_call x0 -> x4, Pallas kernels: none -> 25.9 us  [the longest x1 15.3 us: project(): pl.pallas_call(project_kernel, out_shape=jax.ShapeDtypeStruct((rows * blo...]
    dot_general x6 -> x0, matrix products: 25.6 us -> none  [the longest x1 7.91 us: per_device(): jnp.einsum('pdju,dus->pdjs', windows, toeplitz, precision=lax.Precision.H...]
    sort x2 -> x0, other arithmetic: 6.33 us -> none  [the longest x1 3.17 us: per_device(): sort_order = jnp.argsort(owners, stable=True)]
    reshape x8 -> x4, local copies, waits for them, and re-layouts: 9.58 us -> 3.41 us  [the longest x2 2.45 us: per_device(): direction.reshape(2, 8, own_patches, PX).transpose(2, 1, 0, 3)]
    gather x5 -> x0, local copies, waits for them, and re-layouts: 5.6 us -> none  [the longest x1 2.18 us: per_device(): partial_value = partial_value[sort_order].reshape(devices, per_owner, width)]
    unnamed x19 -> x33, local copies, waits for them, and re-layouts: 2.32 us -> 7.66 us
    ppermute x2, waiting for transfers between devices: 0.01 us -> 3.74 us  [the longest x1 3.74 us: per_device(): after = lax.ppermute(head, 'tm', [(i + 1, i) for i in range(spans - 1)])]
    all_to_all x1, waiting for transfers between devices: 22.2 us -> 24.6 us  [per_device(): lax.all_to_all(served, ('det', 'tm'), split_axis=0, concat_axis=0, tiled=...]
  transfers between devices with their start and end apart: 5 -> 5, of which waited for: 3 -> 4; matrix products, arithmetic and copies ran while one was open for 8% -> 3% of each run, Pallas kernels for 0% -> 0%
where the time goes in v2:
time: 134 us
  waiting for transfers between devices  58.7 us (44%)
  Pallas kernels  35.5 us (26%)
  starting transfers between devices  19.4 us (14%)
  local copies, waits for them, and re-layouts  14.8 us (11%)
  other arithmetic  4.3 us (3%)
    all_to_all x1, waiting for transfers between devices, per_device(): lax.all_to_all(parts.reshape(devices, per_owner, 8, 128), ('det', 'tm'),...  26.1 us
    all_to_all x1, waiting for transfers between devices, per_device(): lax.all_to_all(served, ('det', 'tm'), split_axis=0, concat_axis=0, tiled=...  24.6 us
    pallas_call x1, Pallas kernels, project(): pl.pallas_call(project_kernel, out_shape=jax.ShapeDtypeStruct((rows * blo...  15.3 us
    pallas_call x1, Pallas kernels, sum_everywhere(): pl.pallas_call(functools.partial(share_kernel, spans, devices), out_shape...  9.65 us
    unnamed x33, local copies, waits for them, and re-layouts  7.66 us
    all_to_all x1, starting transfers between devices, per_device(): lax.all_to_all(requests, ('det', 'tm'), split_axis=0, concat_axis=0, tile...  7.3 us
    all_to_all x1, starting transfers between devices, per_device(): lax.all_to_all(parts.reshape(devices, per_owner, 8, 128), ('det', 'tm'),...  6.7 us
    pallas_call x1, Pallas kernels, scan(): pl.pallas_call(scan_kernel, out_shape=(jax.ShapeDtypeStruct((rows, 16 * b...  5.29 us
  transfers between devices with their start and end apart: 5, of which 4 were waited for; matrix products, arithmetic and copies ran while one was open for 3% of the time, Pallas kernels for 0%

profile of v2, /device:TPU:0, one launch (start us, length us, event | category | flops | bytes accessed | tf_op | source)
XLA Modules:
  0.0 133.5 jit_solution(8596071883570395681)
XLA Ops:
  2.5 7.3 %all-to-all-start = ((s32[32,1,8]{2,1,0:T(1,128)}), s32[32,1,8]{2,1,0:T(1,128)S(1)}, u32[]{:S(2)}, u32[]{:S(2)}) async-start(s32[32,1,8]{2,1,0:T(1,128)} %bitcast.1), calls=%async_computation | async-start | bytes 32768 | tf_op jit(solution)/shard_map/all_to_all | solution.py:239
  9.8 1.5 %reshape.183 = f32[2,8,128,64]{3,2,1,0:T(8,128)S(1)} reshape(f32[16,8192]{1,0:T(8,128)} %param.11) | data formatting | bytes 1048576 | tf_op jit(solution)/shard_map/reshape | solution.py:242
  11.6 1.0 copy.34.table_ref
  12.6 4.3 %all-to-all-done = s32[32,1,8]{2,1,0:T(1,128)S(1)} async-done(((s32[32,1,8]{2,1,0:T(1,128)}), s32[32,1,8]{2,1,0:T(1,128)S(1)}, u32[]{:S(2)}, u32[]{:S(2)}) %all-to-all-start) | async-done | bytes 1056 | tf_op jit(solution)/shard_map/all_to_all | solution.py:239
  18.7 2.5 %shard_map.112 = f32[256,8,128]{2,1,0:T(8,128)} custom-call(s32[256]{0:T(256)} %reshape.182.asked_ref, f32[128,8,128]{2,1,0:T(8,128)} %copy.34.table_ref), custom_call_target="tpu_custom_call" | custom-call | tf_op jit(solution)/shard_map/pallas_call | solution.py:34
  21.2 2.8 %all-to-all-start.1 = ((f32[32,8,8,128]{3,2,1,0:T(8,128)}), f32[32,8,8,128]{3,2,1,0:T(8,128)S(1)}, u32[]{:S(2)}, u32[]{:S(2)}) async-start(f32[32,8,8,128]{3,2,1,0:T(8,128)} %bitcast.45), calls=%async_computation.1 | async-start | bytes 2097152 | tf_op jit(solution)/shard_map/all_to_all | solution.py:245
  25.6 24.6 %all-to-all-done.1 = f32[32,8,8,128]{3,2,1,0:T(8,128)S(1)} async-done(((f32[32,8,8,128]{3,2,1,0:T(8,128)}), f32[32,8,8,128]{3,2,1,0:T(8,128)S(1)}, u32[]{:S(2)}, u32[]{:S(2)}) %all-to-all-start.1) | async-done | bytes 1048608 | tf_op jit(solution)/shard_map/all_to_all | solution.py:245
  50.2 1.0 copy-done.6
  51.2 5.3 %shard_map.113 = (f32[32,128,128]{2,1,0:T(8,128)}, f32[16,16,128]{2,1,0:T(8,128)}, f32[16,16,128]{2,1,0:T(8,128)}) custom-call(s32[256]{0:T(256)} %copy-done.3, f32[256,8,128]{2,1,0:T(8,128)} %bitcast.44, s32[32,8,128]{2,1,0:T(8,128)} %bitcast.37, f32[32,8,128]{2,1,0:T(8,128)} %bitcast.39), custom_call_target="tpu_custom_call" | custom-call | tf_op jit(solution)/shard_map/pallas_call | solution.py:97
  56.5 1.3 collective-permute-start
  57.8 1.3 collective-permute-start.1
  59.2 3.7 %collective-permute-done.1.after_ref = f32[16,16,128]{2,1,0:T(8,128)S(1)} collective-permute-done((f32[16,16,128]{2,1,0:T(8,128)}, f32[16,16,128]{2,1,0:T(8,128)S(1)}, u32[]{:S(2)}, u32[]{:S(2)}) %collective-permute-start.1) | collective-permute-done | bytes 131104 | tf_op jit(solution)/shard_map/ppermute | solution.py:250
  62.9 1.6 %copy-done = f32[32,128,128]{2,1,0:T(8,128)S(1)} copy-done((f32[32,128,128]{2,1,0:T(8,128)S(1)}, f32[32,128,128]{2,1,0:T(8,128)}, u32[]{:S(2)}) %copy-start) | copy-done | bytes 2097176
  64.5 0.9 copy-done.1
  65.4 0.9 copy-done.2
  66.3 15.3 %shard_map.114 = f32[256,8,128]{2,1,0:T(8,128)} custom-call(s32[256]{0:T(256)S(1)} %copy-done.4, f32[32,128,128]{2,1,0:T(8,128)S(1)} %copy-done, f32[16,16,128]{2,1,0:T(8,128)S(1)} %collective-permute-done.before_ref, f32[16,16,128]{2,1,0:T(8,128)S(1)} %collective-permute-done.1.after_ref, f32[32,1,256]{2,1,0:T(1,128)S(1)} %broadcast_in_dim.22.base_ref, ...), custom_call_target="tpu_custom_call" | custom-call | tf_op jit(solution)/shard_map/pallas_call | solution.py:156
  81.6 6.7 %all-to-all-start.2 = ((f32[32,8,8,128]{3,2,1,0:T(8,128)}), f32[32,8,8,128]{3,2,1,0:T(8,128)S(1)}, u32[]{:S(2)}, u32[]{:S(2)}) async-start(f32[32,8,8,128]{3,2,1,0:T(8,128)} %bitcast.7), calls=%async_computation.2 | async-start | bytes 2097152 | tf_op jit(solution)/shard_map/all_to_all | solution.py:261
  88.5 26.1 %all-to-all-done.2 = f32[32,8,8,128]{3,2,1,0:T(8,128)S(1)} async-done(((f32[32,8,8,128]{3,2,1,0:T(8,128)}), f32[32,8,8,128]{3,2,1,0:T(8,128)S(1)}, u32[]{:S(2)}, u32[]{:S(2)}) %all-to-all-start.2) | async-done | bytes 1048608 | tf_op jit(solution)/shard_map/all_to_all | solution.py:261
  114.6 1.0 copy-done.7
  115.5 2.8 %shard_map.115 = f32[128,8,128]{2,1,0:T(8,128)} custom-call(s32[256]{0:T(256)} %reshape.182.asked_ref, f32[256,8,128]{2,1,0:T(8,128)} %bitcast.46), custom_call_target="tpu_custom_call" | custom-call | tf_op jit(solution)/shard_map/pallas_call | solution.py:53
  118.4 1.2 copy.36
  121.7 9.6 %shard_map.116 = f32[8,128]{1,0:T(8,128)} custom-call(f32[8,128]{1,0:T(8,128)} %select_maximum_fusion.part_ref), custom_call_target="tpu_custom_call" | custom-call | tf_op jit(solution)/shard_map/pallas_call | solution.py:205
  131.4 0.8 subtract_divide_fusion
  132.2 1.3 multiply_add_fusion
  (54 shorter events, 8.0 us)
Async XLA Ops:
  1.7 10.9 %copy-start.3 = (s32[256]{0:T(256)}, s32[256]{0:T(256)S(1)}, u32[]{:S(2)}) copy-start(s32[256]{0:T(256)S(1)} %multiply_add_fusion.2.slot_ref) | copy-start | bytes 3076
  2.5 14.4 %all-to-all-start = ((s32[32,1,8]{2,1,0:T(1,128)}), s32[32,1,8]{2,1,0:T(1,128)S(1)}, u32[]{:S(2)}, u32[]{:S(2)}) async-start(s32[32,1,8]{2,1,0:T(1,128)} %bitcast.1), calls=%async_computation | async-start | bytes 32768 | tf_op jit(solution)/shard_map/all_to_all | solution.py:239
  12.6 11.4 %copy-start.11 = (s32[32,1024]{1,0:T(8,128)S(1)}, s32[32,1024]{1,0:T(8,128)}, u32[]{:S(2)}) copy-start(s32[32,1024]{1,0:T(8,128)} %param.14) | copy-start | bytes 393220
  12.6 12.1 %copy-start.12 = (f32[32,1024]{1,0:T(8,128)S(1)}, f32[32,1024]{1,0:T(8,128)}, u32[]{:S(2)}) copy-start(f32[32,1024]{1,0:T(8,128)} %param.15) | copy-start | bytes 393220
  18.7 6.7 %copy-start.14 = (f32[32]{0:T(128)S(1)}, f32[32]{0:T(128)}, u32[]{:S(2)}) copy-start(f32[32]{0:T(128)} %param.16) | copy-start | bytes 388
  18.7 6.8 %copy-start.13 = (f32[32,64]{1,0:T(8,128)S(1)}, f32[32,64]{1,0:T(8,128)}, u32[]{:S(2)}) copy-start(f32[32,64]{1,0:T(8,128)} %param.17) | copy-start | bytes 24580
  21.2 41.7 %copy-start.4 = (s32[256]{0:T(256)S(1)}, s32[256]{0:T(256)}, u32[]{:S(2)}) copy-start(s32[256]{0:T(256)} %copy-done.3) | copy-start | bytes 3076
  21.2 29.0 %all-to-all-start.1 = ((f32[32,8,8,128]{3,2,1,0:T(8,128)}), f32[32,8,8,128]{3,2,1,0:T(8,128)S(1)}, u32[]{:S(2)}, u32[]{:S(2)}) async-start(f32[32,8,8,128]{3,2,1,0:T(8,128)} %bitcast.45), calls=%async_computation.1 | async-start | bytes 2097152 | tf_op jit(solution)/shard_map/all_to_all | solution.py:245
  50.2 1.0 copy-start.6
  56.5 2.7 %collective-permute-start = (f32[16,16,128]{2,1,0:T(8,128)}, f32[16,16,128]{2,1,0:T(8,128)S(1)}, u32[]{:S(2)}, u32[]{:S(2)}) collective-permute-start(f32[16,16,128]{2,1,0:T(8,128)} %get-tuple-element.7), channel_id=1, source_target_pairs={{0,1},{1,2},{2,3},{3,4},{4,5},{5,6},{6,7},{8,9},{9,10},{10,11},{11... | collective-permute-start | bytes 393224 | tf_op jit(solution)/shard_map/ppermute | solution.py:249
  57.8 5.2 %collective-permute-start.1 = (f32[16,16,128]{2,1,0:T(8,128)}, f32[16,16,128]{2,1,0:T(8,128)S(1)}, u32[]{:S(2)}, u32[]{:S(2)}) collective-permute-start(f32[16,16,128]{2,1,0:T(8,128)} %get-tuple-element.8), channel_id=1, source_target_pairs={{1,0},{2,1},{3,2},{4,3},{5,4},{6,5},{7,6},{9,8},{10,9},{11,10},{12... | collective-permute-start | bytes 393224 | tf_op jit(solution)/shard_map/ppermute | solution.py:250
  62.9 1.6 %copy-start = (f32[32,128,128]{2,1,0:T(8,128)S(1)}, f32[32,128,128]{2,1,0:T(8,128)}, u32[]{:S(2)}) copy-start(f32[32,128,128]{2,1,0:T(8,128)} %get-tuple-element.6.line_ref) | copy-start | bytes 6291460
  64.5 0.9 copy-start.1
  65.4 0.9 copy-start.2
  66.3 22.0 %copy-start.10 = (f32[8192]{0:T(1024)S(1)}, f32[8192]{0:T(1024)}, u32[]{:S(2)}) copy-start(f32[8192]{0:T(1024)} %param.12) | copy-start | bytes 98308
  81.6 32.9 %all-to-all-start.2 = ((f32[32,8,8,128]{3,2,1,0:T(8,128)}), f32[32,8,8,128]{3,2,1,0:T(8,128)S(1)}, u32[]{:S(2)}, u32[]{:S(2)}) async-start(f32[32,8,8,128]{3,2,1,0:T(8,128)} %bitcast.7), calls=%async_computation.2 | async-start | bytes 2097152 | tf_op jit(solution)/shard_map/all_to_all | solution.py:261
  114.6 1.0 copy-start.7
  119.6 1.1 copy-start.5
  119.6 1.2 copy-start.8
  120.3 11.9 %copy-start.9 = (f32[16,8192]{1,0:T(8,128)S(1)}, f32[16,8192]{1,0:T(8,128)}, u32[]{:S(2)}) copy-start(f32[16,8192]{1,0:T(8,128)} %param.9) | copy-start | bytes 1572868

commit v3 on v2

--- a/solution.py
+++ b/solution.py
@@ -1,4 +1,5 @@
 import functools
+import math
 
 import jax
 import jax.numpy as jnp
@@ -23,20 +24,150 @@
     return pl.BlockSpec(memory_space=pltpu.SMEM)
 
 
-def serve_kernel(asked_ref, table_ref, out_ref):
-    @pl.loop(0, out_ref.shape[0], step=8)
-    def _(first):
-        for i in range(8):
-            out_ref[first + i] = table_ref[asked_ref[first + i]]
-
-
-def serve(asked, table):
-    return pl.pallas_call(
-        serve_kernel,
-        out_shape=jax.ShapeDtypeStruct(asked.shape + table.shape[1:], jnp.float32),
-        in_specs=[smem()] + vmem(1),
+def peers_of(spans, devices):
+    me = lax.axis_index("det") * spans + lax.axis_index("tm")
+    stride = spans + 1 if math.gcd(spans + 1, devices) == 1 else 1
+
+    def ahead(step):
+        return lax.rem(me + step * stride, devices)
+
+    def behind(step):
+        return lax.rem(me + (devices - step) * stride, devices)
+
+    def place(peer):
+        return (peer // spans, lax.rem(peer, spans))
+
+    return me, ahead, behind, place
+
+
+def remote(src, dst, sent, got, device):
+    return pltpu.make_async_remote_copy(
+        src_ref=src,
+        dst_ref=dst,
+        send_sem=sent,
+        recv_sem=got,
+        device_id=device,
+        device_id_type=pl.DeviceIdType.MESH,
+    )
+
+
+def greet(devices, ahead, place):
+    barrier = pltpu.get_barrier_semaphore()
+
+    @pl.loop(1, devices)
+    def _(step):
+        pl.semaphore_signal(
+            barrier, inc=1, device_id=place(ahead(step)), device_id_type=pl.DeviceIdType.MESH
+        )
+
+    pl.semaphore_wait(barrier, devices - 1)
+
+
+def fetch_kernel(
+    spans, devices, ask_ref, table_ref, asked_ref, out_ref,
+    served, numbers, ask_sent, ask_got, sent, got, local,
+):
+    me, ahead, behind, place = peers_of(spans, devices)
+    per_owner = out_ref.shape[1]
+    greet(devices, ahead, place)
+
+    def ask(step, slot):
+        peer = ahead(step)
+        return remote(
+            ask_ref.at[peer], asked_ref.at[slot], ask_sent.at[step], ask_got.at[step], place(peer)
+        )
+
+    def give(step, slot):
+        peer = ahead(step)
+        return remote(
+            served.at[peer], out_ref.at[slot], sent.at[step], got.at[step], place(peer)
+        )
+
+    @pl.loop(1, devices)
+    def _(step):
+        ask(step, me).start()
+
+    asked_ref[me] = ask_ref[me]
+
+    @pl.loop(1, devices)
+    def _(step):
+        ask(step, behind(step)).wait_recv()
+
+    move = pltpu.make_async_copy(asked_ref, numbers, local)
+    move.start()
+    move.wait()
+
+    @pl.loop(1, devices)
+    def _(step):
+        peer = ahead(step)
+        for i in range(per_owner):
+            served[peer, i] = table_ref[numbers[peer, 0, i]]
+        give(step, me).start()
+
+    for i in range(per_owner):
+        out_ref[me, i] = table_ref[numbers[me, 0, i]]
+
+    @pl.loop(1, devices)
+    def _(step):
+        ask(step, me).wait_send()
+        give(step, me).wait_send()
+        give(step, behind(step)).wait_recv()
+
+
+def fetch(ask, table, per_owner, spans, devices):
+    return pl.pallas_call(
+        functools.partial(fetch_kernel, spans, devices),
+        out_shape=(
+            jax.ShapeDtypeStruct(ask.shape, jnp.int32),
+            jax.ShapeDtypeStruct((devices, per_owner, 8, 128), jnp.float32),
+        ),
+        in_specs=vmem(2),
+        out_specs=tuple(vmem(2)),
+        scratch_shapes=[
+            pltpu.VMEM((devices, per_owner, 8, 128), jnp.float32),
+            pltpu.SMEM(ask.shape, jnp.int32),
+        ]
+        + [pltpu.SemaphoreType.DMA((devices,))] * 4
+        + [pltpu.SemaphoreType.DMA],
+        compiler_params=pltpu.CompilerParams(
+            collective_id=1, has_side_effects=True, vmem_limit_bytes=32 * 1024 * 1024
+        ),
+    )(ask, table)
+
+
+def swap_kernel(spans, devices, part_ref, out_ref, sent, got):
+    me, ahead, behind, place = peers_of(spans, devices)
+    greet(devices, ahead, place)
+
+    def give(step, slot):
+        peer = ahead(step)
+        return remote(
+            part_ref.at[peer], out_ref.at[slot], sent.at[step], got.at[step], place(peer)
+        )
+
+    @pl.loop(1, devices)
+    def _(step):
+        give(step, me).start()
+
+    out_ref[me] = part_ref[me]
+
+    @pl.loop(1, devices)
+    def _(step):
+        give(step, me).wait_send()
+        give(step, behind(step)).wait_recv()
+
+
+def swap(parts, spans, devices):
+    return pl.pallas_call(
+        functools.partial(swap_kernel, spans, devices),
+        out_shape=jax.ShapeDtypeStruct(parts.shape, jnp.float32),
+        in_specs=vmem(1),
         out_specs=vmem(1)[0],
-    )(asked, table)
+        scratch_shapes=[pltpu.SemaphoreType.DMA((devices,))] * 2,
+        compiler_params=pltpu.CompilerParams(
+            collective_id=2, has_side_effects=True, vmem_limit_bytes=32 * 1024 * 1024
+        ),
+    )(parts)
 
 
 def gather_up_kernel(asked_ref, parts_ref, out_ref):
@@ -236,13 +367,12 @@
     requests = jnp.sum(
         jnp.where(numbers[:, None] == slot[None, :], (patch_flat % own_patches)[None, :], 0), axis=1
     ).reshape(devices, per_owner)
-    asked = lax.all_to_all(requests, ("det", "tm"), split_axis=0, concat_axis=0, tiled=True)
-    asked = asked.reshape(blocks)
+    requests = jnp.pad(requests, ((0, 0), (0, 128 - per_owner)))[:, None, :]
     table = (
         direction.reshape(2, 8, own_patches, PX).transpose(2, 1, 0, 3).reshape(own_patches, 8, 128)
     )
-    served = serve(asked, table).reshape(devices, per_owner, 8, 128)
-    fetched = lax.all_to_all(served, ("det", "tm"), split_axis=0, concat_axis=0, tiled=True)
+    asked, fetched = fetch(requests, table, per_owner, spans, devices)
+    asked = asked[:, 0, :per_owner].reshape(blocks)
     pixels = pixel_in.reshape(det_rows, time_blocks, 128)
     gains = weights.reshape(det_rows, time_blocks, 128)
     line, head, tail = scan(slot, fetched.reshape(blocks, 8, 128), pixels, gains)
@@ -258,13 +388,8 @@
         axis=1,
     )[:, None, :]
     parts = project(slot, line, before, after, base, pixels, gains)
-    collected = lax.all_to_all(
-        parts.reshape(devices, per_owner, 8, 128),
-        ("det", "tm"),
-        split_axis=0,
-        concat_axis=0,
-        tiled=True,
-    ).reshape(blocks, 8, 128)
+    collected = swap(parts.reshape(devices, per_owner, 8, 128), spans, devices)
+    collected = collected.reshape(blocks, 8, 128)
     image_map = (
         gather_up(asked, collected, own_patches)
         .reshape(own_patches, 8, 2, PX)

time: 134 us -> 123 us (0.918)
  Pallas kernels: 35.5 us -> 102 us
  waiting for transfers between devices: 58.7 us -> 2.66 us
  starting transfers between devices: 19.4 us -> 2.58 us
  local copies, waits for them, and re-layouts: 14.8 us -> 11.2 us
    pallas_call x1 -> x2, Pallas kernels: 2.5 us -> 69.4 us  [the longest x1 37.6 us: fetch(): pl.pallas_call(functools.partial(fetch_kernel, spans, devices), out_shape...]
    all_to_all x3 -> x0, waiting for transfers between devices: 55 us -> none  [the longest x1 26.1 us: per_device(): lax.all_to_all(parts.reshape(devices, per_owner, 8, 128), ('det', 'tm'),...]
    all_to_all x3 -> x0, starting transfers between devices: 16.8 us -> none  [the longest x1 7.3 us: per_device(): lax.all_to_all(requests, ('det', 'tm'), split_axis=0, concat_axis=0, tile...]
    unnamed x33, local copies, waits for them, and re-layouts: 7.66 us -> 5.87 us
  transfers between devices with their start and end apart: 5 -> 2, of which waited for: 4 -> 1; matrix products, arithmetic and copies ran while one was open for 3% -> 1% of each run, Pallas kernels for 0% -> 0%
where the time goes in v3:
time: 123 us
  Pallas kernels  102 us (83%)
  local copies, waits for them, and re-layouts  11.2 us (9%)
  other arithmetic  3.62 us (3%)
  waiting for transfers between devices  2.66 us (2%)
  starting transfers between devices  2.58 us (2%)
    pallas_call x1, Pallas kernels, fetch(): pl.pallas_call(functools.partial(fetch_kernel, spans, devices), out_shape...  37.6 us
    pallas_call x1, Pallas kernels, swap(): pl.pallas_call(functools.partial(swap_kernel, spans, devices), out_shape=...  31.8 us
    pallas_call x1, Pallas kernels, project(): pl.pallas_call(project_kernel, out_shape=jax.ShapeDtypeStruct((rows * blo...  14.3 us
    pallas_call x1, Pallas kernels, sum_everywhere(): pl.pallas_call(functools.partial(share_kernel, spans, devices), out_shape...  10.2 us
    unnamed x33, local copies, waits for them, and re-layouts  5.87 us
    pallas_call x1, Pallas kernels, scan(): pl.pallas_call(scan_kernel, out_shape=(jax.ShapeDtypeStruct((rows, 16 * b...  5.29 us
    pallas_call x1, Pallas kernels, gather_up(): pl.pallas_call(gather_up_kernel, out_shape=jax.ShapeDtypeStruct((rows,) +...  2.84 us
    ppermute x1, waiting for transfers between devices, per_device(): after = lax.ppermute(head, 'tm', [(i + 1, i) for i in range(spans - 1)])  2.64 us
  transfers between devices with their start and end apart: 2, of which 1 were waited for; matrix products, arithmetic and copies ran while one was open for 1% of the time, Pallas kernels for 0%

profile of v3, /device:TPU:0, one launch (start us, length us, event | category | flops | bytes accessed | tf_op | source)
XLA Modules:
  0.0 123.1 jit_solution(6458984091618508801)
XLA Ops:
  0.6 0.8 copy.30
  1.9 1.5 %reshape.175 = f32[2,8,128,64]{3,2,1,0:T(8,128)S(1)} reshape(f32[16,8192]{1,0:T(8,128)} %param.11) | data formatting | bytes 1048576 | tf_op jit(solution)/shard_map/reshape | solution.py:372
  4.1 0.7 copy.38
  4.7 0.7 copy.39
  5.4 37.6 %shard_map.112 = (s32[32,1,128]{2,1,0:T(1,128)S(1)}, f32[32,8,8,128]{3,2,1,0:T(8,128)S(1)}) custom-call(s32[32,1,128]{2,1,0:T(1,128)S(1)} %bitcast.43, f32[128,8,128]{2,1,0:T(8,128)S(1)} %copy.32.table_ref), custom_call_target="tpu_custom_call" | custom-call | tf_op jit(solution)/shard_map/pallas_call | solution.py:118
  43.0 1.0 copy-done.4
  44.0 5.3 %shard_map.113 = (f32[32,128,128]{2,1,0:T(8,128)}, f32[16,16,128]{2,1,0:T(8,128)}, f32[16,16,128]{2,1,0:T(8,128)}) custom-call(s32[256]{0:T(256)} %copy-done.5, f32[256,8,128]{2,1,0:T(8,128)} %bitcast.42, s32[32,8,128]{2,1,0:T(8,128)} %bitcast.38, f32[32,8,128]{2,1,0:T(8,128)} %bitcast.40), custom_call_target="tpu_custom_call" | custom-call | tf_op jit(solution)/shard_map/pallas_call | solution.py:228
  49.3 1.3 %collective-permute-start = (f32[16,16,128]{2,1,0:T(8,128)}, f32[16,16,128]{2,1,0:T(8,128)S(1)}, u32[]{:S(2)}, u32[]{:S(2)}) collective-permute-start(f32[16,16,128]{2,1,0:T(8,128)} %get-tuple-element.11), channel_id=1, source_target_pairs={{0,1},{1,2},{2,3},{3,4},{4,5},{5,6},{6,7},{8,9},{9,10},{10,11},{11... | collective-permute-start | bytes 393224 | tf_op jit(solution)/shard_map/ppermute | solution.py:379
  50.6 1.3 %collective-permute-start.1 = (f32[16,16,128]{2,1,0:T(8,128)}, f32[16,16,128]{2,1,0:T(8,128)S(1)}, u32[]{:S(2)}, u32[]{:S(2)}) collective-permute-start(f32[16,16,128]{2,1,0:T(8,128)} %get-tuple-element.12), channel_id=1, source_target_pairs={{1,0},{2,1},{3,2},{4,3},{5,4},{6,5},{7,6},{9,8},{10,9},{11,10},{12... | collective-permute-start | bytes 393224 | tf_op jit(solution)/shard_map/ppermute | solution.py:380
  52.0 0.6 reshape_squeeze.3.asked_ref
  53.1 2.6 %collective-permute-done.1.after_ref = f32[16,16,128]{2,1,0:T(8,128)S(1)} collective-permute-done((f32[16,16,128]{2,1,0:T(8,128)}, f32[16,16,128]{2,1,0:T(8,128)S(1)}, u32[]{:S(2)}, u32[]{:S(2)}) %collective-permute-start.1) | collective-permute-done | bytes 131104 | tf_op jit(solution)/shard_map/ppermute | solution.py:380
  55.8 1.6 %copy-done.1 = f32[32,128,128]{2,1,0:T(8,128)S(1)} copy-done((f32[32,128,128]{2,1,0:T(8,128)S(1)}, f32[32,128,128]{2,1,0:T(8,128)}, u32[]{:S(2)}) %copy-start.1) | copy-done | bytes 2097176
  57.3 14.3 %shard_map.114 = f32[256,8,128]{2,1,0:T(8,128)S(1)} custom-call(s32[256]{0:T(256)S(1)} %copy-done.6, f32[32,128,128]{2,1,0:T(8,128)S(1)} %copy-done.1, f32[16,16,128]{2,1,0:T(8,128)S(1)} %collective-permute-done.before_ref, f32[16,16,128]{2,1,0:T(8,128)S(1)} %collective-permute-done.1.after_ref, f32[32,1,256]{2,1,0:T(1,128)S(1)} %broadcast_in_dim.42.base_ref, ...), custom_call_target="tpu_custom_call" | custom-call | tf_op jit(solution)/shard_map/pallas_call | solution.py:287
  71.6 31.8 %shard_map.115 = f32[32,8,8,128]{3,2,1,0:T(8,128)S(1)} custom-call(f32[32,8,8,128]{3,2,1,0:T(8,128)S(1)} %bitcast.37), custom_call_target="tpu_custom_call" | custom-call | tf_op jit(solution)/shard_map/pallas_call | solution.py:161
  103.5 1.0 copy-done
  104.4 2.8 %shard_map.116 = f32[128,8,128]{2,1,0:T(8,128)} custom-call(s32[256]{0:T(256)} %reshape_squeeze.3.asked_ref, f32[256,8,128]{2,1,0:T(8,128)} %bitcast.36), custom_call_target="tpu_custom_call" | custom-call | tf_op jit(solution)/shard_map/pallas_call | solution.py:184
  107.3 1.2 %copy.34 = f32[128,8,128]{0,2,1:T(8,128)S(1)} copy(f32[128,8,128]{2,1,0:T(8,128)} %shard_map.116) | data formatting | bytes 1048576 | tf_op jit(solution)/shard_map/pallas_call | solution.py:184
  108.5 0.3 copy.35
  109.2 0.4 reshape.183
  109.7 0.3 fusion
  110.0 0.6 select_maximum_fusion.part_ref
  110.6 10.2 %shard_map.117 = f32[8,128]{1,0:T(8,128)} custom-call(f32[8,128]{1,0:T(8,128)} %select_maximum_fusion.part_ref), custom_call_target="tpu_custom_call" | custom-call | tf_op jit(solution)/shard_map/pallas_call | solution.py:336
  120.9 0.8 subtract_divide_fusion
  121.7 1.3 %multiply_add_fusion = (f32[16,8192]{1,0:T(8,128)}, f32[16,8192]{1,0:T(8,128)}, f32[16,8192]{1,0:T(8,128)}) fusion(f32[16,8192]{1,0:T(8,128)S(1)} %copy-done.7, f32[16]{0:T(128)S(1)} %get-tuple-element.18, f32[8192]{0:T(1024)S(1)} %copy-done.10, f32[16,8192]{1,0:T(8,128)S(1)} %copy-done.8, f32[16,8192]{1,0:T(8,128)S(1)} %reshape.183, ...), kind=kLoop, calls=%fused_computation.6 | loop fusion | flops 917504 | bytes 3702912 | tf_op jit(solution)/shard_map/add | solution.py:417
  (49 shorter events, 2.1 us)
Async XLA Ops:
  1.7 2.3 %copy-start.5 = (s32[256]{0:T(256)}, s32[256]{0:T(256)S(1)}, u32[]{:S(2)}) copy-start(s32[256]{0:T(256)S(1)} %multiply_add_fusion.2.slot_ref) | copy-start | bytes 3076
  1.9 2.1 %copy-start.11 = (s32[32,1024]{1,0:T(8,128)S(1)}, s32[32,1024]{1,0:T(8,128)}, u32[]{:S(2)}) copy-start(s32[32,1024]{1,0:T(8,128)} %param.14) | copy-start | bytes 393220
  1.9 2.8 %copy-start.12 = (f32[32,1024]{1,0:T(8,128)S(1)}, f32[32,1024]{1,0:T(8,128)}, u32[]{:S(2)}) copy-start(f32[32,1024]{1,0:T(8,128)} %param.15) | copy-start | bytes 393220
  3.8 48.8 %copy-start.13 = (f32[32,64]{1,0:T(8,128)S(1)}, f32[32,64]{1,0:T(8,128)}, u32[]{:S(2)}) copy-start(f32[32,64]{1,0:T(8,128)} %param.17) | copy-start | bytes 24580
  3.8 48.9 %copy-start.14 = (f32[32]{0:T(128)S(1)}, f32[32]{0:T(128)}, u32[]{:S(2)}) copy-start(f32[32]{0:T(128)} %param.16) | copy-start | bytes 388
  3.8 49.1 %copy-start.10 = (f32[8192]{0:T(1024)S(1)}, f32[8192]{0:T(1024)}, u32[]{:S(2)}) copy-start(f32[8192]{0:T(1024)} %param.12) | copy-start | bytes 98308
  4.1 51.7 %copy-start.6 = (s32[256]{0:T(256)S(1)}, s32[256]{0:T(256)}, u32[]{:S(2)}) copy-start(s32[256]{0:T(256)} %copy-done.5) | copy-start | bytes 3076
  4.7 51.0 %copy-start.2 = (s32[4,8,8,128]{3,2,1,0:T(8,128)S(1)}, s32[4,8,8,128]{3,2,1,0:T(8,128)}, u32[]{:S(2)}) copy-start(s32[4,8,8,128]{3,2,1,0:T(8,128)} %copy.38) | copy-start | bytes 393220
  5.4 50.3 %copy-start.3 = (f32[4,8,8,128]{3,2,1,0:T(8,128)S(1)}, f32[4,8,8,128]{3,2,1,0:T(8,128)}, u32[]{:S(2)}) copy-start(f32[4,8,8,128]{3,2,1,0:T(8,128)} %copy.39) | copy-start | bytes 393220
  43.0 1.0 copy-start.4
  49.3 3.8 %collective-permute-start = (f32[16,16,128]{2,1,0:T(8,128)}, f32[16,16,128]{2,1,0:T(8,128)S(1)}, u32[]{:S(2)}, u32[]{:S(2)}) collective-permute-start(f32[16,16,128]{2,1,0:T(8,128)} %get-tuple-element.11), channel_id=1, source_target_pairs={{0,1},{1,2},{2,3},{3,4},{4,5},{5,6},{6,7},{8,9},{9,10},{10,11},{11... | collective-permute-start | bytes 393224 | tf_op jit(solution)/shard_map/ppermute | solution.py:379
  50.6 5.1 %collective-permute-start.1 = (f32[16,16,128]{2,1,0:T(8,128)}, f32[16,16,128]{2,1,0:T(8,128)S(1)}, u32[]{:S(2)}, u32[]{:S(2)}) collective-permute-start(f32[16,16,128]{2,1,0:T(8,128)} %get-tuple-element.12), channel_id=1, source_target_pairs={{1,0},{2,1},{3,2},{4,3},{5,4},{6,5},{7,6},{9,8},{10,9},{11,10},{12... | collective-permute-start | bytes 393224 | tf_op jit(solution)/shard_map/ppermute | solution.py:380
  55.8 1.6 %copy-start.1 = (f32[32,128,128]{2,1,0:T(8,128)S(1)}, f32[32,128,128]{2,1,0:T(8,128)}, u32[]{:S(2)}) copy-start(f32[32,128,128]{2,1,0:T(8,128)} %get-tuple-element.10.line_ref) | copy-start | bytes 6291460
  103.5 1.0 copy-start
  108.5 1.1 copy-start.7
  108.5 1.2 copy-start.8
  108.9 12.9 %copy-start.9 = (f32[16,8192]{1,0:T(8,128)S(1)}, f32[16,8192]{1,0:T(8,128)}, u32[]{:S(2)}) copy-start(f32[16,8192]{1,0:T(8,128)} %param.9) | copy-start | bytes 1572868

commit v4 on v3

--- a/solution.py
+++ b/solution.py
@@ -170,14 +170,22 @@
     )(parts)
 
 
-def gather_up_kernel(asked_ref, parts_ref, out_ref):
-    out_ref[...] = jnp.zeros_like(out_ref)
-
-    @pl.loop(0, parts_ref.shape[0], step=8)
-    def _(first):
-        for i in range(8):
-            row = asked_ref[first + i]
-            out_ref[row] = out_ref[row] + parts_ref[first + i]
+def gather_up_kernel(asked_ref, parts_ref, out_ref, *others):
+    chains = (out_ref,) + others
+    share = parts_ref.shape[0] // len(chains)
+    for chain in chains:
+        chain[...] = jnp.zeros_like(chain)
+
+    @pl.loop(0, share, unroll=4)
+    def _(i):
+        for c, chain in enumerate(chains):
+            row = asked_ref[c * share + i]
+            chain[row] = chain[row] + parts_ref[c * share + i]
+
+    total = out_ref[...]
+    for chain in others:
+        total = total + chain[...]
+    out_ref[...] = total
 
 
 def gather_up(asked, parts, rows):
@@ -186,6 +194,7 @@
         out_shape=jax.ShapeDtypeStruct((rows,) + parts.shape[1:], jnp.float32),
         in_specs=[smem()] + vmem(1),
         out_specs=vmem(1)[0],
+        scratch_shapes=[pltpu.VMEM((rows,) + parts.shape[1:], jnp.float32)] * 3,
     )(asked, parts)
 
 
@@ -196,30 +205,25 @@
 
     def one_row(d):
         pixels, gains = pixel_ref[d], gain_ref[d]
+        ends = []
         for j in range(blocks):
             pixel = jnp.broadcast_to(pixels[j : j + 1], (8, 128))
             gain = jnp.broadcast_to(gains[j : j + 1], (8, 128))
             patch = patches_ref[slot_ref[d * blocks + j]]
-            line_ref[d, 16 * j : 16 * j + 8] = (
-                jnp.take_along_axis(patch, pixel, axis=1) * gain
-            )
-            line_ref[d, 16 * j + 8 : 16 * j + 16] = (
-                jnp.take_along_axis(patch, pixel + 64, axis=1) * gain
-            )
-
-    @pl.loop(0, half)
+            upper = jnp.take_along_axis(patch, pixel, axis=1) * gain
+            lower = jnp.take_along_axis(patch, pixel + 64, axis=1) * gain
+            line_ref[d, 16 * j : 16 * j + 8] = upper
+            line_ref[d, 16 * j + 8 : 16 * j + 16] = lower
+            if j in (0, blocks - 1):
+                ends.append(jnp.concatenate([upper, lower], axis=0))
+        return ends[0], ends[-1]
+
+    @pl.loop(0, half, unroll=2)
     def _(d):
-        one_row(d)
-        one_row(d + half)
-        last = 16 * (blocks - 1)
-        head_ref[d] = jnp.where(
-            left, line_ref[d, 0:16], pltpu.roll(line_ref[d + half, 0:16], 64, 1)
-        )
-        tail_ref[d] = jnp.where(
-            left,
-            pltpu.roll(line_ref[d + half, last : last + 16], 64, 1),
-            line_ref[d, last : last + 16],
-        )
+        first, last = one_row(d)
+        later_first, later_last = one_row(d + half)
+        head_ref[d] = jnp.where(left, first, pltpu.roll(later_first, 64, 1))
+        tail_ref[d] = jnp.where(left, pltpu.roll(later_last, 64, 1), last)
 
 
 def scan(slot, patches, pixel, gain):
@@ -275,7 +279,7 @@
             added = added[:16] + added[16:]
             out_ref[slot_ref[d * blocks + j]] = jnp.concatenate([added[:8], added[8:]], axis=1)
 
-    @pl.loop(0, half)
+    @pl.loop(0, half, unroll=2)
     def _(d):
         before, after = before_ref[d], after_ref[d]
         one_row(d, before, after)
@@ -293,58 +297,72 @@
     )(slot, line, before, after, base, pixel, gain)
 
 
-def share_kernel(spans, devices, part_ref, out_ref, held, send_sem, recv_sem):
-    me = lax.axis_index("det") * spans + lax.axis_index("tm")
+def factors_kernel(
+    spans, devices, old_ref, way_ref, scale_ref, image_ref, out_ref, part, held, sent, got
+):
+    me, ahead, behind, place = peers_of(spans, devices)
     barrier = pltpu.get_barrier_semaphore()
 
-    def place(step):
-        peer = lax.rem(me + step, devices)
-        return (peer // spans, lax.rem(peer, spans))
-
-    def copy_to(step):
-        return pltpu.make_async_remote_copy(
-            src_ref=part_ref,
-            dst_ref=held.at[step],
-            send_sem=send_sem.at[step],
-            recv_sem=recv_sem.at[step],
-            device_id=place(step),
-            device_id_type=pl.DeviceIdType.MESH,
-        )
-
     @pl.loop(1, devices)
     def _(step):
         pl.semaphore_signal(
-            barrier, inc=1, device_id=place(step), device_id_type=pl.DeviceIdType.MESH
-        )
-
+            barrier, inc=1, device_id=place(ahead(step)), device_id_type=pl.DeviceIdType.MESH
+        )
+
+    image = image_ref[...]
+    lean = scale_ref[...] * old_ref[...]
+    columns = (
+        jnp.sum(old_ref[...] * lean, axis=1, keepdims=True),
+        jnp.sum(way_ref[...] * image, axis=1, keepdims=True),
+        jnp.sum(image * lean, axis=1, keepdims=True),
+        jnp.sum(image * (scale_ref[...] * image), axis=1, keepdims=True),
+    )
+    lane = lax.broadcasted_iota(jnp.int32, part.shape, 1)
+    tile = jnp.zeros(part.shape, jnp.float32)
+    for i, column in enumerate(columns):
+        tile = jnp.where(lane == i, column, tile)
+    part[...] = tile
+    held[me] = tile
     pl.semaphore_wait(barrier, devices - 1)
 
-    @pl.loop(1, devices)
-    def _(step):
-        copy_to(step).start()
-
-    held[0] = part_ref[...]
-
-    @pl.loop(1, devices)
-    def _(step):
-        copy_to(step).wait()
-
-    out_ref[...] = jnp.sum(held[...], axis=0)
-
-
-def sum_everywhere(part, spans, devices):
-    return pl.pallas_call(
-        functools.partial(share_kernel, spans, devices),
-        out_shape=jax.ShapeDtypeStruct(part.shape, jnp.float32),
-        in_specs=[pl.BlockSpec(memory_space=pltpu.VMEM)],
-        out_specs=pl.BlockSpec(memory_space=pltpu.VMEM),
+    def give(step, slot):
+        return remote(
+            part, held.at[slot], sent.at[step], got.at[step], place(ahead(step))
+        )
+
+    @pl.loop(1, devices)
+    def _(step):
+        give(step, me).start()
+
+    @pl.loop(1, devices)
+    def _(step):
+        give(step, me).wait_send()
+        give(step, behind(step)).wait_recv()
+
+    total = jnp.sum(held[...], axis=0)
+    norm_old, curvature, cross, square = (total[:, i : i + 1] for i in range(4))
+    step_size = norm_old / curvature
+    norm_new = norm_old - step_size * (2.0 * cross - step_size * square)
+    out_ref[...] = jnp.where(lane == 0, step_size, norm_new / norm_old)
+
+
+def factors(residual, direction, precond, image, spans, devices):
+    tile = (residual.shape[0], 128)
+    return pl.pallas_call(
+        functools.partial(factors_kernel, spans, devices),
+        out_shape=jax.ShapeDtypeStruct(tile, jnp.float32),
+        in_specs=vmem(4),
+        out_specs=vmem(1)[0],
         scratch_shapes=[
-            pltpu.VMEM((devices,) + part.shape, jnp.float32),
+            pltpu.VMEM(tile, jnp.float32),
+            pltpu.VMEM((devices,) + tile, jnp.float32),
             pltpu.SemaphoreType.DMA((devices,)),
             pltpu.SemaphoreType.DMA((devices,)),
         ],
-        compiler_params=pltpu.CompilerParams(collective_id=0, has_side_effects=True),
-    )(part)
+        compiler_params=pltpu.CompilerParams(
+            collective_id=0, has_side_effects=True, vmem_limit_bytes=32 * 1024 * 1024
+        ),
+    )(residual, direction, precond, image)
 
 
 def per_device(
@@ -396,25 +414,11 @@
         .transpose(2, 1, 0, 3)
         .reshape(probes, own_patches * PX)
     )
-    lean = precond * residual
-    drop = precond * image_map
-    sums = jnp.stack(
-        [
-            jnp.sum(residual * lean, axis=1),
-            jnp.sum(direction * image_map, axis=1),
-            jnp.sum(image_map * lean, axis=1),
-            jnp.sum(image_map * drop, axis=1),
-        ]
-    )
-    part = jnp.pad(sums, ((0, 4), (0, 128 - probes)))
-    total = sum_everywhere(part, spans, devices)
-    norm_old, curvature, cross, square = (total[i, :probes] for i in range(4))
-    step_size = norm_old / curvature
-    norm_new = norm_old - step_size * (2.0 * cross - step_size * square)
-    new_iterate = iterate + step_size[:, None] * direction
-    new_residual = residual - step_size[:, None] * image_map
-    scaled = precond * new_residual
-    new_direction = scaled + (norm_new / norm_old)[:, None] * direction
+    factor = factors(residual, direction, precond[None, :], image_map, spans, devices)
+    step_size, ratio = factor[:, 0:1], factor[:, 1:2]
+    new_iterate = iterate + step_size * direction
+    new_residual = residual - step_size * image_map
+    new_direction = precond * new_residual + ratio * direction
     return (new_iterate, new_residual, new_direction)
 
 

time: 123 us -> 121 us (0.984)
  other arithmetic: 3.62 us -> 1.7 us
    pallas_call x1, Pallas kernels: 10.2 us -> 12.9 us  [factors(): pl.pallas_call(functools.partial(factors_kernel, spans, devices), out_sha...]
    pallas_call x1, Pallas kernels: 14.3 us -> 11.9 us  [project(): pl.pallas_call(project_kernel, out_shape=jax.ShapeDtypeStruct((rows * blo...]
where the time goes in v4:
time: 121 us
  Pallas kernels  102 us (84%)
  local copies, waits for them, and re-layouts  11.1 us (9%)
  waiting for transfers between devices  2.74 us (2%)
  starting transfers between devices  2.58 us (2%)
  other arithmetic  1.7 us (1%)
    pallas_call x1, Pallas kernels, fetch(): pl.pallas_call(functools.partial(fetch_kernel, spans, devices), out_shape...  37.6 us
    pallas_call x1, Pallas kernels, swap(): pl.pallas_call(functools.partial(swap_kernel, spans, devices), out_shape=...  31.8 us
    pallas_call x1, Pallas kernels, factors(): pl.pallas_call(functools.partial(factors_kernel, spans, devices), out_sha...  12.9 us
    pallas_call x1, Pallas kernels, project(): pl.pallas_call(project_kernel, out_shape=jax.ShapeDtypeStruct((rows * blo...  11.9 us
    unnamed x33, local copies, waits for them, and re-layouts  5.71 us
    pallas_call x1, Pallas kernels, scan(): pl.pallas_call(scan_kernel, out_shape=(jax.ShapeDtypeStruct((rows, 16 * b...  4.78 us
    ppermute x1, waiting for transfers between devices, per_device(): after = lax.ppermute(head, 'tm', [(i + 1, i) for i in range(spans - 1)])  2.74 us
    pallas_call x1, Pallas kernels, gather_up(): pl.pallas_call(gather_up_kernel, out_shape=jax.ShapeDtypeStruct((rows,) +...  2.65 us
  transfers between devices with their start and end apart: 2, of which 1 were waited for; matrix products, arithmetic and copies ran while one was open for 1% of the time, Pallas kernels for 0%

profile of v4, /device:TPU:0, one launch (start us, length us, event | category | flops | bytes accessed | tf_op | source)
XLA Modules:
  0.0 120.6 jit_solution(13892568357038101392)
XLA Ops:
  0.6 0.8 copy.21
  1.5 0.2 convert_reduce_fusion
  1.9 1.5 %reshape.132 = f32[2,8,128,64]{3,2,1,0:T(8,128)S(1)} reshape(f32[16,8192]{1,0:T(8,128)} %way_ref.1) | data formatting | bytes 1048576 | tf_op jit(solution)/shard_map/reshape | solution.py:390
  3.4 0.3 copy.22
  3.8 0.2 copy.23.table_ref
  4.0 0.7 copy.27
  4.7 0.7 copy.28
  5.4 37.6 %shard_map.112 = (s32[32,1,128]{2,1,0:T(1,128)S(1)}, f32[32,8,8,128]{3,2,1,0:T(8,128)S(1)}) custom-call(s32[32,1,128]{2,1,0:T(1,128)S(1)} %bitcast.25, f32[128,8,128]{2,1,0:T(8,128)S(1)} %copy.23.table_ref), custom_call_target="tpu_custom_call" | custom-call | tf_op jit(solution)/shard_map/pallas_call | solution.py:118
  43.0 1.0 copy-done.6
  44.0 4.8 %shard_map.113 = (f32[32,128,128]{2,1,0:T(8,128)}, f32[16,16,128]{2,1,0:T(8,128)}, f32[16,16,128]{2,1,0:T(8,128)}) custom-call(s32[256]{0:T(256)} %copy-done.8, f32[256,8,128]{2,1,0:T(8,128)} %bitcast.23, s32[32,8,128]{2,1,0:T(8,128)} %bitcast.19, f32[32,8,128]{2,1,0:T(8,128)} %bitcast.21), custom_call_target="tpu_custom_call" | custom-call | tf_op jit(solution)/shard_map/pallas_call | solution.py:232
  48.8 1.3 %collective-permute-start = (f32[16,16,128]{2,1,0:T(8,128)}, f32[16,16,128]{2,1,0:T(8,128)S(1)}, u32[]{:S(2)}, u32[]{:S(2)}) collective-permute-start(f32[16,16,128]{2,1,0:T(8,128)} %get-tuple-element.11), channel_id=1, source_target_pairs={{0,1},{1,2},{2,3},{3,4},{4,5},{5,6},{6,7},{8,9},{9,10},{10,11},{11... | collective-permute-start | bytes 393224 | tf_op jit(solution)/shard_map/ppermute | solution.py:397
  50.1 1.3 %collective-permute-start.1 = (f32[16,16,128]{2,1,0:T(8,128)}, f32[16,16,128]{2,1,0:T(8,128)S(1)}, u32[]{:S(2)}, u32[]{:S(2)}) collective-permute-start(f32[16,16,128]{2,1,0:T(8,128)} %get-tuple-element.12), channel_id=1, source_target_pairs={{1,0},{2,1},{3,2},{4,3},{5,4},{6,5},{7,6},{9,8},{10,9},{11,10},{12... | collective-permute-start | bytes 393224 | tf_op jit(solution)/shard_map/ppermute | solution.py:398
  51.4 0.7 reshape_squeeze.3.asked_ref
  52.5 2.7 %collective-permute-done.1.after_ref = f32[16,16,128]{2,1,0:T(8,128)S(1)} collective-permute-done((f32[16,16,128]{2,1,0:T(8,128)}, f32[16,16,128]{2,1,0:T(8,128)S(1)}, u32[]{:S(2)}, u32[]{:S(2)}) %collective-permute-start.1) | collective-permute-done | bytes 131104 | tf_op jit(solution)/shard_map/ppermute | solution.py:398
  55.2 1.6 %copy-done.2 = f32[32,128,128]{2,1,0:T(8,128)S(1)} copy-done((f32[32,128,128]{2,1,0:T(8,128)S(1)}, f32[32,128,128]{2,1,0:T(8,128)}, u32[]{:S(2)}) %copy-start.2) | copy-done | bytes 2097176
  56.8 11.9 %shard_map.114 = f32[256,8,128]{2,1,0:T(8,128)S(1)} custom-call(s32[256]{0:T(256)S(1)} %copy-done.9, f32[32,128,128]{2,1,0:T(8,128)S(1)} %copy-done.2, f32[16,16,128]{2,1,0:T(8,128)S(1)} %collective-permute-done.before_ref, f32[16,16,128]{2,1,0:T(8,128)S(1)} %collective-permute-done.1.after_ref, f32[32,1,256]{2,1,0:T(1,128)S(1)} %broadcast_in_dim.41.base_ref, ...), custom_call_target="tpu_custom_call" | custom-call | tf_op jit(solution)/shard_map/pallas_call | solution.py:291
  68.7 31.8 %shard_map.115 = f32[32,8,8,128]{3,2,1,0:T(8,128)S(1)} custom-call(f32[32,8,8,128]{3,2,1,0:T(8,128)S(1)} %bitcast.18), custom_call_target="tpu_custom_call" | custom-call | tf_op jit(solution)/shard_map/pallas_call | solution.py:161
  100.5 1.0 copy-done.1
  101.5 2.7 %shard_map.116 = f32[128,8,128]{2,1,0:T(8,128)} custom-call(s32[256]{0:T(256)} %reshape_squeeze.3.asked_ref, f32[256,8,128]{2,1,0:T(8,128)} %bitcast.17), custom_call_target="tpu_custom_call" | custom-call | tf_op jit(solution)/shard_map/pallas_call | solution.py:192
  104.1 1.3 %copy.25 = f32[128,8,128]{0,2,1:T(8,128)S(1)} copy(f32[128,8,128]{2,1,0:T(8,128)} %shard_map.116) | data formatting | bytes 1048576 | tf_op jit(solution)/shard_map/pallas_call | solution.py:192
  105.5 0.3 copy.26
  105.8 0.4 reshape.140.image_ref
  106.2 12.9 %shard_map.117 = f32[16,128]{1,0:T(8,128)S(1)} custom-call(f32[16,8192]{1,0:T(8,128)S(1)} %copy-done.3, f32[16,8192]{1,0:T(8,128)S(1)} %copy-done, f32[1,8192]{1,0:T(1,128)S(1)} %bitcast.24, f32[16,8192]{1,0:T(8,128)S(1)} %reshape.140.image_ref), custom_call_target="tpu_custom_call" | custom-call | tf_op jit(solution)/shard_map/pallas_call | solution.py:351
  119.3 1.3 %multiply_add_fusion = (f32[16,8192]{1,0:T(8,128)}, f32[16,8192]{1,0:T(8,128)}, f32[16,8192]{1,0:T(8,128)}) fusion(f32[16,8192]{1,0:T(8,128)S(1)} %copy-done, f32[16]{0:T(128)S(1)} %get-tuple-element.13, f32[8192]{0:T(1024)S(1)} %copy-done.7, f32[16,8192]{1,0:T(8,128)S(1)} %copy-done.3, f32[16,8192]{1,0:T(8,128)S(1)} %reshape.140.image_ref, ...), kind=kLoop, calls=%fused_computation | loop fusion | flops 917504 | bytes 3702912 | tf_op jit(solution)/shard_map/add | solution.py:421
  (42 shorter events, 0.9 us)
Async XLA Ops:
  1.7 2.3 %copy-start.8 = (s32[256]{0:T(256)}, s32[256]{0:T(256)S(1)}, u32[]{:S(2)}) copy-start(s32[256]{0:T(256)S(1)} %multiply_add_fusion.2.slot_ref) | copy-start | bytes 3076
  1.9 2.1 %copy-start.11 = (s32[32,1024]{1,0:T(8,128)S(1)}, s32[32,1024]{1,0:T(8,128)}, u32[]{:S(2)}) copy-start(s32[32,1024]{1,0:T(8,128)} %param.14) | copy-start | bytes 393220
  1.9 2.8 %copy-start.12 = (f32[32,1024]{1,0:T(8,128)S(1)}, f32[32,1024]{1,0:T(8,128)}, u32[]{:S(2)}) copy-start(f32[32,1024]{1,0:T(8,128)} %param.15) | copy-start | bytes 393220
  3.8 48.3 %copy-start.13 = (f32[32,64]{1,0:T(8,128)S(1)}, f32[32,64]{1,0:T(8,128)}, u32[]{:S(2)}) copy-start(f32[32,64]{1,0:T(8,128)} %param.17) | copy-start | bytes 24580
  3.8 48.4 %copy-start.14 = (f32[32]{0:T(128)S(1)}, f32[32]{0:T(128)}, u32[]{:S(2)}) copy-start(f32[32]{0:T(128)} %param.16) | copy-start | bytes 388
  4.0 51.2 %copy-start.9 = (s32[256]{0:T(256)S(1)}, s32[256]{0:T(256)}, u32[]{:S(2)}) copy-start(s32[256]{0:T(256)} %copy-done.8) | copy-start | bytes 3076
  4.7 50.5 %copy-start.4 = (s32[4,8,8,128]{3,2,1,0:T(8,128)S(1)}, s32[4,8,8,128]{3,2,1,0:T(8,128)}, u32[]{:S(2)}) copy-start(s32[4,8,8,128]{3,2,1,0:T(8,128)} %copy.27) | copy-start | bytes 393220
  5.4 49.8 %copy-start.5 = (f32[4,8,8,128]{3,2,1,0:T(8,128)S(1)}, f32[4,8,8,128]{3,2,1,0:T(8,128)}, u32[]{:S(2)}) copy-start(f32[4,8,8,128]{3,2,1,0:T(8,128)} %copy.28) | copy-start | bytes 393220
  43.0 1.0 copy-start.6
  48.8 3.7 %collective-permute-start = (f32[16,16,128]{2,1,0:T(8,128)}, f32[16,16,128]{2,1,0:T(8,128)S(1)}, u32[]{:S(2)}, u32[]{:S(2)}) collective-permute-start(f32[16,16,128]{2,1,0:T(8,128)} %get-tuple-element.11), channel_id=1, source_target_pairs={{0,1},{1,2},{2,3},{3,4},{4,5},{5,6},{6,7},{8,9},{9,10},{10,11},{11... | collective-permute-start | bytes 393224 | tf_op jit(solution)/shard_map/ppermute | solution.py:397
  50.1 5.1 %collective-permute-start.1 = (f32[16,16,128]{2,1,0:T(8,128)}, f32[16,16,128]{2,1,0:T(8,128)S(1)}, u32[]{:S(2)}, u32[]{:S(2)}) collective-permute-start(f32[16,16,128]{2,1,0:T(8,128)} %get-tuple-element.12), channel_id=1, source_target_pairs={{1,0},{2,1},{3,2},{4,3},{5,4},{6,5},{7,6},{9,8},{10,9},{11,10},{12... | collective-permute-start | bytes 393224 | tf_op jit(solution)/shard_map/ppermute | solution.py:398
  55.2 1.6 %copy-start.2 = (f32[32,128,128]{2,1,0:T(8,128)S(1)}, f32[32,128,128]{2,1,0:T(8,128)}, u32[]{:S(2)}) copy-start(f32[32,128,128]{2,1,0:T(8,128)} %get-tuple-element.10.line_ref) | copy-start | bytes 6291460
  100.5 1.0 copy-start.1
  104.1 2.1 %copy-start = (f32[16,8192]{1,0:T(8,128)S(1)}, f32[16,8192]{1,0:T(8,128)}, u32[]{:S(2)}) copy-start(f32[16,8192]{1,0:T(8,128)} %way_ref.1) | copy-start | bytes 1572868
  104.1 2.1 %copy-start.3 = (f32[16,8192]{1,0:T(8,128)S(1)}, f32[16,8192]{1,0:T(8,128)}, u32[]{:S(2)}) copy-start(f32[16,8192]{1,0:T(8,128)} %old_ref.1) | copy-start | bytes 1572868
  104.1 2.1 %copy-start.7 = (f32[8192]{0:T(1024)S(1)}, f32[8192]{0:T(1024)}, u32[]{:S(2)}) copy-start(f32[8192]{0:T(1024)} %param.12) | copy-start | bytes 98308
  105.4 13.8 %copy-start.10 = (f32[16,8192]{1,0:T(8,128)S(1)}, f32[16,8192]{1,0:T(8,128)}, u32[]{:S(2)}) copy-start(f32[16,8192]{1,0:T(8,128)} %param.9) | copy-start | bytes 1572868

commit v5 on v4

--- a/solution.py
+++ b/solution.py
@@ -64,11 +64,15 @@
 
 
 def fetch_kernel(
-    spans, devices, ask_ref, table_ref, asked_ref, out_ref,
-    served, numbers, ask_sent, ask_got, sent, got, local,
+    spans, devices, slot_ref, ask_ref, table_ref, pixel_ref, gain_ref,
+    asked_ref, line_ref, before_ref, after_ref,
+    served, patches, numbers, head, tail,
+    ask_sent, ask_got, sent, got, local, edge_sent, edge_got,
 ):
     me, ahead, behind, place = peers_of(spans, devices)
-    per_owner = out_ref.shape[1]
+    per_owner = served.shape[1]
+    rows, blocks, _ = pixel_ref.shape
+    half = rows // 2
     greet(devices, ahead, place)
 
     def ask(step, slot):
@@ -80,7 +84,11 @@
     def give(step, slot):
         peer = ahead(step)
         return remote(
-            served.at[peer], out_ref.at[slot], sent.at[step], got.at[step], place(peer)
+            served.at[peer],
+            patches.at[pl.ds(slot * per_owner, per_owner)],
+            sent.at[step],
+            got.at[step],
+            place(peer),
         )
 
     @pl.loop(1, devices)
@@ -105,7 +113,7 @@
         give(step, me).start()
 
     for i in range(per_owner):
-        out_ref[me, i] = table_ref[numbers[me, 0, i]]
+        patches[me * per_owner + i] = table_ref[numbers[me, 0, i]]
 
     @pl.loop(1, devices)
     def _(step):
@@ -113,26 +121,85 @@
         give(step, me).wait_send()
         give(step, behind(step)).wait_recv()
 
-
-def fetch(ask, table, per_owner, spans, devices):
+    left = lax.broadcasted_iota(jnp.int32, (16, 128), 1) < 64
+
+    def scan(d, wanted):
+        pixels, gains = pixel_ref[d], gain_ref[d]
+        made = []
+        for j in wanted:
+            pixel = jnp.broadcast_to(pixels[j : j + 1], (8, 128))
+            gain = jnp.broadcast_to(gains[j : j + 1], (8, 128))
+            patch = patches[slot_ref[d * blocks + j]]
+            upper = jnp.take_along_axis(patch, pixel, axis=1) * gain
+            lower = jnp.take_along_axis(patch, pixel + 64, axis=1) * gain
+            line_ref[d, 16 * j : 16 * j + 8] = upper
+            line_ref[d, 16 * j + 8 : 16 * j + 16] = lower
+            made.append(jnp.concatenate([upper, lower], axis=0))
+        return made
+
+    @pl.loop(0, half)
+    def _(d):
+        first, last = scan(d, (0, blocks - 1))
+        later_first, later_last = scan(d + half, (0, blocks - 1))
+        head[d] = jnp.where(left, first, pltpu.roll(later_first, 64, 1))
+        tail[d] = jnp.where(left, pltpu.roll(later_last, 64, 1), last)
+
+    span = lax.axis_index("tm")
+    group = lax.axis_index("det")
+    forth = remote(
+        tail, before_ref, edge_sent.at[0], edge_got.at[0],
+        (group, lax.rem(span + 1, spans)),
+    )
+    back = remote(
+        head, after_ref, edge_sent.at[1], edge_got.at[1],
+        (group, lax.rem(span + spans - 1, spans)),
+    )
+    forth.start()
+    back.start()
+
+    @pl.loop(0, rows)
+    def _(d):
+        scan(d, range(1, blocks - 1))
+
+    forth.wait()
+    back.wait()
+
+    @pl.when(span == 0)
+    def _():
+        before_ref[...] = jnp.zeros_like(before_ref)
+
+    @pl.when(span == spans - 1)
+    def _():
+        after_ref[...] = jnp.zeros_like(after_ref)
+
+
+def fetch(slot, ask, table, pixels, gains, per_owner, spans, devices):
+    rows, blocks, _ = pixels.shape
+    edge = (rows // 2, 16, 128)
     return pl.pallas_call(
         functools.partial(fetch_kernel, spans, devices),
         out_shape=(
             jax.ShapeDtypeStruct(ask.shape, jnp.int32),
-            jax.ShapeDtypeStruct((devices, per_owner, 8, 128), jnp.float32),
+            jax.ShapeDtypeStruct((rows, 16 * blocks, 128), jnp.float32),
+            jax.ShapeDtypeStruct(edge, jnp.float32),
+            jax.ShapeDtypeStruct(edge, jnp.float32),
         ),
-        in_specs=vmem(2),
-        out_specs=tuple(vmem(2)),
+        in_specs=[smem()] + vmem(4),
+        out_specs=tuple(vmem(4)),
         scratch_shapes=[
             pltpu.VMEM((devices, per_owner, 8, 128), jnp.float32),
+            pltpu.VMEM((devices * per_owner, 8, 128), jnp.float32),
             pltpu.SMEM(ask.shape, jnp.int32),
+            pltpu.VMEM(edge, jnp.float32),
+            pltpu.VMEM(edge, jnp.float32),
         ]
         + [pltpu.SemaphoreType.DMA((devices,))] * 4
-        + [pltpu.SemaphoreType.DMA],
+        + [pltpu.SemaphoreType.DMA]
+        + [pltpu.SemaphoreType.DMA((2,))] * 2,
         compiler_params=pltpu.CompilerParams(
             collective_id=1, has_side_effects=True, vmem_limit_bytes=32 * 1024 * 1024
         ),
-    )(ask, table)
+    )(slot, ask, table, pixels, gains)
 
 
 def swap_kernel(spans, devices, part_ref, out_ref, sent, got):
@@ -196,45 +263,6 @@
         out_specs=vmem(1)[0],
         scratch_shapes=[pltpu.VMEM((rows,) + parts.shape[1:], jnp.float32)] * 3,
     )(asked, parts)
-
-
-def scan_kernel(slot_ref, patches_ref, pixel_ref, gain_ref, line_ref, head_ref, tail_ref):
-    rows, blocks, _ = pixel_ref.shape
-    half = rows // 2
-    left = lax.broadcasted_iota(jnp.int32, (16, 128), 1) < 64
-
-    def one_row(d):
-        pixels, gains = pixel_ref[d], gain_ref[d]
-        ends = []
-        for j in range(blocks):
-            pixel = jnp.broadcast_to(pixels[j : j + 1], (8, 128))
-            gain = jnp.broadcast_to(gains[j : j + 1], (8, 128))
-            patch = patches_ref[slot_ref[d * blocks + j]]
-            upper = jnp.take_along_axis(patch, pixel, axis=1) * gain
-            lower = jnp.take_along_axis(patch, pixel + 64, axis=1) * gain
-            line_ref[d, 16 * j : 16 * j + 8] = upper
-            line_ref[d, 16 * j + 8 : 16 * j + 16] = lower
-            if j in (0, blocks - 1):
-                ends.append(jnp.concatenate([upper, lower], axis=0))
-        return ends[0], ends[-1]
-
-    @pl.loop(0, half, unroll=2)
-    def _(d):
-        first, last = one_row(d)
-        later_first, later_last = one_row(d + half)
-        head_ref[d] = jnp.where(left, first, pltpu.roll(later_first, 64, 1))
-        tail_ref[d] = jnp.where(left, pltpu.roll(later_last, 64, 1), last)
-
-
-def scan(slot, patches, pixel, gain):
-    rows, blocks, _ = pixel.shape
-    edge = jax.ShapeDtypeStruct((rows // 2, 16, 128), jnp.float32)
-    return pl.pallas_call(
-        scan_kernel,
-        out_shape=(jax.ShapeDtypeStruct((rows, 16 * blocks, 128), jnp.float32), edge, edge),
-        in_specs=[smem()] + vmem(3),
-        out_specs=tuple(vmem(3)),
-    )(slot, patches, pixel, gain)
 
 
 def project_kernel(
@@ -389,13 +417,12 @@
     table = (
         direction.reshape(2, 8, own_patches, PX).transpose(2, 1, 0, 3).reshape(own_patches, 8, 128)
     )
-    asked, fetched = fetch(requests, table, per_owner, spans, devices)
-    asked = asked[:, 0, :per_owner].reshape(blocks)
     pixels = pixel_in.reshape(det_rows, time_blocks, 128)
     gains = weights.reshape(det_rows, time_blocks, 128)
-    line, head, tail = scan(slot, fetched.reshape(blocks, 8, 128), pixels, gains)
-    before = lax.ppermute(tail, "tm", [(i, i + 1) for i in range(spans - 1)])
-    after = lax.ppermute(head, "tm", [(i + 1, i) for i in range(spans - 1)])
+    asked, line, before, after = fetch(
+        slot, requests, table, pixels, gains, per_owner, spans, devices
+    )
+    asked = asked[:, 0, :per_owner].reshape(blocks)
     base = jnp.concatenate(
         [
             filter_diag[:, None],

time: 121 us -> 114 us (0.942)
  waiting for transfers between devices: 2.74 us -> 0 us
  starting transfers between devices: 2.58 us -> 0 us
  Pallas kernels: 102 us -> 99.9 us
    pallas_call x1, Pallas kernels: 37.6 us -> 44.5 us  [fetch(): pl.pallas_call(functools.partial(fetch_kernel, spans, devices), out_shape...]
    pallas_call x1 -> x0, Pallas kernels: 4.78 us -> none  [scan(): pl.pallas_call(scan_kernel, out_shape=(jax.ShapeDtypeStruct((rows, 16 * b...]
    pallas_call x1, Pallas kernels: 31.8 us -> 28.2 us  [swap(): pl.pallas_call(functools.partial(swap_kernel, spans, devices), out_shape=...]
    ppermute x2 -> x0, waiting for transfers between devices: 2.74 us -> none  [the longest x1 2.74 us: per_device(): after = lax.ppermute(head, 'tm', [(i + 1, i) for i in range(spans - 1)])]
    ppermute x2 -> x0, starting transfers between devices: 2.58 us -> none  [the longest x1 1.29 us: per_device(): after = lax.ppermute(head, 'tm', [(i + 1, i) for i in range(spans - 1)])]
    unnamed x33 -> x13, local copies, waits for them, and re-layouts: 5.71 us -> 3.62 us
  transfers between devices with their start and end apart: 2 -> 0, of which waited for: 1 -> 0; matrix products, arithmetic and copies ran while one was open for 1% -> 0% of each run, Pallas kernels for 0% -> 0%
where the time goes in v5:
time: 114 us; the launch traced here: 113 us
  Pallas kernels  99.9 us (88%)
  local copies, waits for them, and re-layouts  10.3 us (9%)
  other arithmetic  2.42 us (2%)
    pallas_call x1, Pallas kernels, fetch(): pl.pallas_call(functools.partial(fetch_kernel, spans, devices), out_shape...  44.5 us
    pallas_call x1, Pallas kernels, swap(): pl.pallas_call(functools.partial(swap_kernel, spans, devices), out_shape=...  28.2 us
    pallas_call x1, Pallas kernels, factors(): pl.pallas_call(functools.partial(factors_kernel, spans, devices), out_sha...  12.7 us
    pallas_call x1, Pallas kernels, project(): pl.pallas_call(project_kernel, out_shape=jax.ShapeDtypeStruct((rows * blo...  11.8 us
    unnamed x13, local copies, waits for them, and re-layouts  3.62 us
    pallas_call x1, Pallas kernels, gather_up(): pl.pallas_call(gather_up_kernel, out_shape=jax.ShapeDtypeStruct((rows,) +...  2.65 us

profile of v5, /device:TPU:0, one launch (start us, length us, event | category | flops | bytes accessed | tf_op | source)
XLA Modules:
  0.0 113.5 jit_solution(4959460961327200575)
XLA Ops:
  0.7 0.8 copy.21
  1.5 0.1 reshape.127
  1.6 0.2 convert_reduce_fusion
  1.8 0.1 select_reduce_fusion
  2.0 0.7 copy.24
  2.7 0.8 rev.3
  3.5 0.8 pad_maximum_fusion
  4.4 0.9 copy.27
  5.3 0.9 copy.28
  6.2 1.5 %reshape.129 = f32[2,8,128,64]{3,2,1,0:T(8,128)S(1)} reshape(f32[16,8192]{1,0:T(8,128)} %way_ref.1) | data formatting | bytes 1048576 | tf_op jit(solution)/shard_map/reshape | solution.py:418
  7.7 0.3 copy.22
  8.0 0.2 copy.23.table_ref
  8.3 44.5 %shard_map.112 = (s32[32,1,128]{2,1,0:T(1,128)S(1)}, f32[32,128,128]{2,1,0:T(8,128)S(1)}, f32[16,16,128]{2,1,0:T(8,128)S(1)}, f32[16,16,128]{2,1,0:T(8,128)S(1)}) custom-call(s32[256]{0:T(256)S(1)} %multiply_add_fusion.2.slot_ref, s32[32,1,128]{2,1,0:T(1,128)S(1)} %bitcast.23, f32[128,8,128]{2,1,0:T(8,128)S(1)} %copy.23.table_ref, ...), custom_call_target="tpu_custom_call" | custom-call | tf_op jit(solution)/shard_map/pallas_call | solution.py:179
  52.8 0.7 reshape_squeeze.3.asked_ref
  53.5 11.8 %shard_map.113 = f32[256,8,128]{2,1,0:T(8,128)S(1)} custom-call(s32[256]{0:T(256)S(1)} %multiply_add_fusion.2.slot_ref, f32[32,128,128]{2,1,0:T(8,128)S(1)} %get-tuple-element.8.line_ref, f32[16,16,128]{2,1,0:T(8,128)S(1)} %get-tuple-element.9.before_ref, f32[16,16,128]{2,1,0:T(8,128)S(1)} %get-tuple-element.10.after_ref, ...), custom_call_target="tpu_custom_call" | custom-call | tf_op jit(solution)/shard_map/pallas_call | solution.py:319
  65.3 28.2 %shard_map.114 = f32[32,8,8,128]{3,2,1,0:T(8,128)S(1)} custom-call(f32[32,8,8,128]{3,2,1,0:T(8,128)S(1)} %bitcast.17), custom_call_target="tpu_custom_call" | custom-call | tf_op jit(solution)/shard_map/pallas_call | solution.py:228
  93.5 1.0 copy-done.1
  94.5 2.7 %shard_map.115 = f32[128,8,128]{2,1,0:T(8,128)} custom-call(s32[256]{0:T(256)} %reshape_squeeze.3.asked_ref, f32[256,8,128]{2,1,0:T(8,128)} %bitcast.16), custom_call_target="tpu_custom_call" | custom-call | tf_op jit(solution)/shard_map/pallas_call | solution.py:259
  97.2 1.3 %copy.25 = f32[128,8,128]{0,2,1:T(8,128)S(1)} copy(f32[128,8,128]{2,1,0:T(8,128)} %shard_map.115) | data formatting | bytes 1048576 | tf_op jit(solution)/shard_map/pallas_call | solution.py:259
  98.5 0.3 copy.26
  98.9 0.4 reshape.136.image_ref
  99.2 12.7 %shard_map.116 = f32[16,128]{1,0:T(8,128)S(1)} custom-call(f32[16,8192]{1,0:T(8,128)S(1)} %copy-done.2, f32[16,8192]{1,0:T(8,128)S(1)} %copy-done, f32[1,8192]{1,0:T(1,128)S(1)} %bitcast.22, f32[16,8192]{1,0:T(8,128)S(1)} %reshape.136.image_ref), custom_call_target="tpu_custom_call" | custom-call | tf_op jit(solution)/shard_map/pallas_call | solution.py:379
  112.0 0.2 slice_reduce_fusion.1
  112.2 1.3 %multiply_add_fusion = (f32[16,8192]{1,0:T(8,128)}, f32[16,8192]{1,0:T(8,128)}, f32[16,8192]{1,0:T(8,128)}) fusion(f32[16,8192]{1,0:T(8,128)S(1)} %copy-done, f32[16]{0:T(128)S(1)} %get-tuple-element.11, f32[8192]{0:T(1024)S(1)} %copy-done.3, f32[16,8192]{1,0:T(8,128)S(1)} %copy-done.2, f32[16,8192]{1,0:T(8,128)S(1)} %reshape.136.image_ref, ...), kind=kLoop, calls=%fused_computation | loop fusion | flops 917504 | bytes 3702912 | tf_op jit(solution)/shard_map/add | solution.py:448
  (17 shorter events, 0.3 us)
Async XLA Ops:
  93.5 1.0 copy-start.1
  97.2 2.1 %copy-start = (f32[16,8192]{1,0:T(8,128)S(1)}, f32[16,8192]{1,0:T(8,128)}, u32[]{:S(2)}) copy-start(f32[16,8192]{1,0:T(8,128)} %way_ref.1) | copy-start | bytes 1572868
  97.2 2.1 %copy-start.2 = (f32[16,8192]{1,0:T(8,128)S(1)}, f32[16,8192]{1,0:T(8,128)}, u32[]{:S(2)}) copy-start(f32[16,8192]{1,0:T(8,128)} %old_ref.1) | copy-start | bytes 1572868
  97.2 2.1 %copy-start.3 = (f32[8192]{0:T(1024)S(1)}, f32[8192]{0:T(1024)}, u32[]{:S(2)}) copy-start(f32[8192]{0:T(1024)} %param.12) | copy-start | bytes 98308
  98.5 13.6 %copy-start.4 = (f32[16,8192]{1,0:T(8,128)S(1)}, f32[16,8192]{1,0:T(8,128)}, u32[]{:S(2)}) copy-start(f32[16,8192]{1,0:T(8,128)} %param.9) | copy-start | bytes 1572868

commit v6 on v5

--- a/solution.py
+++ b/solution.py
@@ -202,67 +202,104 @@
     )(slot, ask, table, pixels, gains)
 
 
-def swap_kernel(spans, devices, part_ref, out_ref, sent, got):
+def settle_kernel(
+    spans, devices, part_ref, asked_ref, way_ref, old_ref, scale_ref,
+    image_ref, out_ref, landed, mine, held, sent, got, sum_sent, sum_got,
+):
     me, ahead, behind, place = peers_of(spans, devices)
+    per_owner = part_ref.shape[0] // devices
+    patches = way_ref.shape[0]
     greet(devices, ahead, place)
 
     def give(step, slot):
         peer = ahead(step)
         return remote(
-            part_ref.at[peer], out_ref.at[slot], sent.at[step], got.at[step], place(peer)
+            part_ref.at[pl.ds(peer * per_owner, per_owner)],
+            landed.at[pl.ds(slot * per_owner, per_owner)],
+            sent.at[step],
+            got.at[step],
+            place(peer),
+        )
+
+    def tell(step, slot):
+        return remote(
+            mine, held.at[slot], sum_sent.at[step], sum_got.at[step], place(ahead(step))
         )
 
     @pl.loop(1, devices)
     def _(step):
         give(step, me).start()
 
-    out_ref[me] = part_ref[me]
+    for i in range(per_owner):
+        landed[me * per_owner + i] = part_ref[me * per_owner + i]
+    rows = lax.broadcasted_iota(jnp.int32, (patches, part_ref.shape[0]), 0)
+    hot = jnp.where(rows == asked_ref[...], 1.0, 0.0).astype(jnp.bfloat16)
+    scale = scale_ref[...]
 
     @pl.loop(1, devices)
     def _(step):
         give(step, me).wait_send()
         give(step, behind(step)).wait_recv()
 
-
-def swap(parts, spans, devices):
+    sums = [[], [], [], []]
+    for r in range(8):
+        top, low = halves(landed[:, r, :])
+        image = jnp.dot(hot, top, preferred_element_type=jnp.float32) + jnp.dot(
+            hot, low, preferred_element_type=jnp.float32
+        )
+        image_ref[:, r, :] = image
+        old = old_ref[:, r, :]
+        lean = scale * old
+        terms = (old * lean, way_ref[:, r, :] * image, image * lean, image * (scale * image))
+        for kept, term in zip(sums, terms):
+            kept.append(jnp.sum(term, axis=0, keepdims=True))
+    tile = jnp.concatenate([row for kept in sums for row in kept], axis=0)
+    mine[...] = tile
+    held[me] = tile
+
+    @pl.loop(1, devices)
+    def _(step):
+        tell(step, me).start()
+
+    @pl.loop(1, devices)
+    def _(step):
+        tell(step, me).wait_send()
+        tell(step, behind(step)).wait_recv()
+
+    total = jnp.sum(held[...], axis=0)
+    lane = lax.broadcasted_iota(jnp.int32, total.shape, 1)
+    sides = (
+        jnp.sum(jnp.where(lane < 64, total, 0.0), axis=1, keepdims=True),
+        jnp.sum(jnp.where(lane < 64, 0.0, total), axis=1, keepdims=True),
+    )
+    for i, side in enumerate(sides):
+        norm_old, curvature, cross, square = (side[8 * q : 8 * q + 8] for q in range(4))
+        step_size = norm_old / curvature
+        norm_new = norm_old - step_size * (2.0 * cross - step_size * square)
+        out_ref[8 * i : 8 * i + 8] = jnp.where(
+            lane[:8] == 0, step_size, norm_new / norm_old
+        )
+
+
+def settle(parts, asked, way, old, scale, spans, devices):
     return pl.pallas_call(
-        functools.partial(swap_kernel, spans, devices),
-        out_shape=jax.ShapeDtypeStruct(parts.shape, jnp.float32),
-        in_specs=vmem(1),
-        out_specs=vmem(1)[0],
-        scratch_shapes=[pltpu.SemaphoreType.DMA((devices,))] * 2,
+        functools.partial(settle_kernel, spans, devices),
+        out_shape=(
+            jax.ShapeDtypeStruct(way.shape, jnp.float32),
+            jax.ShapeDtypeStruct((16, 128), jnp.float32),
+        ),
+        in_specs=vmem(5),
+        out_specs=tuple(vmem(2)),
+        scratch_shapes=[
+            pltpu.VMEM(parts.shape, jnp.float32),
+            pltpu.VMEM((32, 128), jnp.float32),
+            pltpu.VMEM((devices, 32, 128), jnp.float32),
+        ]
+        + [pltpu.SemaphoreType.DMA((devices,))] * 4,
         compiler_params=pltpu.CompilerParams(
             collective_id=2, has_side_effects=True, vmem_limit_bytes=32 * 1024 * 1024
         ),
-    )(parts)
-
-
-def gather_up_kernel(asked_ref, parts_ref, out_ref, *others):
-    chains = (out_ref,) + others
-    share = parts_ref.shape[0] // len(chains)
-    for chain in chains:
-        chain[...] = jnp.zeros_like(chain)
-
-    @pl.loop(0, share, unroll=4)
-    def _(i):
-        for c, chain in enumerate(chains):
-            row = asked_ref[c * share + i]
-            chain[row] = chain[row] + parts_ref[c * share + i]
-
-    total = out_ref[...]
-    for chain in others:
-        total = total + chain[...]
-    out_ref[...] = total
-
-
-def gather_up(asked, parts, rows):
-    return pl.pallas_call(
-        gather_up_kernel,
-        out_shape=jax.ShapeDtypeStruct((rows,) + parts.shape[1:], jnp.float32),
-        in_specs=[smem()] + vmem(1),
-        out_specs=vmem(1)[0],
-        scratch_shapes=[pltpu.VMEM((rows,) + parts.shape[1:], jnp.float32)] * 3,
-    )(asked, parts)
+    )(parts, asked, way, old, scale)
 
 
 def project_kernel(
@@ -323,74 +360,6 @@
         out_specs=vmem(1)[0],
         compiler_params=pltpu.CompilerParams(vmem_limit_bytes=40 * 1024 * 1024),
     )(slot, line, before, after, base, pixel, gain)
-
-
-def factors_kernel(
-    spans, devices, old_ref, way_ref, scale_ref, image_ref, out_ref, part, held, sent, got
-):
-    me, ahead, behind, place = peers_of(spans, devices)
-    barrier = pltpu.get_barrier_semaphore()
-
-    @pl.loop(1, devices)
-    def _(step):
-        pl.semaphore_signal(
-            barrier, inc=1, device_id=place(ahead(step)), device_id_type=pl.DeviceIdType.MESH
-        )
-
-    image = image_ref[...]
-    lean = scale_ref[...] * old_ref[...]
-    columns = (
-        jnp.sum(old_ref[...] * lean, axis=1, keepdims=True),
-        jnp.sum(way_ref[...] * image, axis=1, keepdims=True),
-        jnp.sum(image * lean, axis=1, keepdims=True),
-        jnp.sum(image * (scale_ref[...] * image), axis=1, keepdims=True),
-    )
-    lane = lax.broadcasted_iota(jnp.int32, part.shape, 1)
-    tile = jnp.zeros(part.shape, jnp.float32)
-    for i, column in enumerate(columns):
-        tile = jnp.where(lane == i, column, tile)
-    part[...] = tile
-    held[me] = tile
-    pl.semaphore_wait(barrier, devices - 1)
-
-    def give(step, slot):
-        return remote(
-            part, held.at[slot], sent.at[step], got.at[step], place(ahead(step))
-        )
-
-    @pl.loop(1, devices)
-    def _(step):
-        give(step, me).start()
-
-    @pl.loop(1, devices)
-    def _(step):
-        give(step, me).wait_send()
-        give(step, behind(step)).wait_recv()
-
-    total = jnp.sum(held[...], axis=0)
-    norm_old, curvature, cross, square = (total[:, i : i + 1] for i in range(4))
-    step_size = norm_old / curvature
-    norm_new = norm_old - step_size * (2.0 * cross - step_size * square)
-    out_ref[...] = jnp.where(lane == 0, step_size, norm_new / norm_old)
-
-
-def factors(residual, direction, precond, image, spans, devices):
-    tile = (residual.shape[0], 128)
-    return pl.pallas_call(
-        functools.partial(factors_kernel, spans, devices),
-        out_shape=jax.ShapeDtypeStruct(tile, jnp.float32),
-        in_specs=vmem(4),
-        out_specs=vmem(1)[0],
-        scratch_shapes=[
-            pltpu.VMEM(tile, jnp.float32),
-            pltpu.VMEM((devices,) + tile, jnp.float32),
-            pltpu.SemaphoreType.DMA((devices,)),
-            pltpu.SemaphoreType.DMA((devices,)),
-        ],
-        compiler_params=pltpu.CompilerParams(
-            collective_id=0, has_side_effects=True, vmem_limit_bytes=32 * 1024 * 1024
-        ),
-    )(residual, direction, precond, image)
 
 
 def per_device(
@@ -414,15 +383,22 @@
         jnp.where(numbers[:, None] == slot[None, :], (patch_flat % own_patches)[None, :], 0), axis=1
     ).reshape(devices, per_owner)
     requests = jnp.pad(requests, ((0, 0), (0, 128 - per_owner)))[:, None, :]
-    table = (
-        direction.reshape(2, 8, own_patches, PX).transpose(2, 1, 0, 3).reshape(own_patches, 8, 128)
-    )
+
+    def tiles(field):
+        return (
+            field.reshape(2, 8, own_patches, PX)
+            .transpose(2, 1, 0, 3)
+            .reshape(own_patches, 8, 128)
+        )
+
+    table = tiles(direction)
+    scale = jnp.tile(precond.reshape(own_patches, PX), (1, 2))
     pixels = pixel_in.reshape(det_rows, time_blocks, 128)
     gains = weights.reshape(det_rows, time_blocks, 128)
     asked, line, before, after = fetch(
         slot, requests, table, pixels, gains, per_owner, spans, devices
     )
-    asked = asked[:, 0, :per_owner].reshape(blocks)
+    asked = asked[:, 0, :per_owner].reshape(1, blocks)
     base = jnp.concatenate(
         [
             filter_diag[:, None],
@@ -433,15 +409,13 @@
         axis=1,
     )[:, None, :]
     parts = project(slot, line, before, after, base, pixels, gains)
-    collected = swap(parts.reshape(devices, per_owner, 8, 128), spans, devices)
-    collected = collected.reshape(blocks, 8, 128)
+    image_tiles, factor = settle(parts, asked, table, tiles(residual), scale, spans, devices)
     image_map = (
-        gather_up(asked, collected, own_patches)
+        image_tiles
         .reshape(own_patches, 8, 2, PX)
         .transpose(2, 1, 0, 3)
         .reshape(probes, own_patches * PX)
     )
-    factor = factors(residual, direction, precond[None, :], image_map, spans, devices)
     step_size, ratio = factor[:, 0:1], factor[:, 1:2]
     new_iterate = iterate + step_size * direction
     new_residual = residual - step_size * image_map

time: 114 us -> 115 us (level)
  Pallas kernels: 99.9 us -> 103 us
  local copies, waits for them, and re-layouts: 10.3 us -> 8.99 us
    pallas_call x3 -> x1, Pallas kernels: 43.5 us -> 46.7 us  [settle(): pl.pallas_call(functools.partial(settle_kernel, spans, devices), out_shap...]
    reshape x3 -> x5, local copies, waits for them, and re-layouts: 2.05 us -> 2.73 us  [the longest x2 1.91 us: tiles(): field.reshape(2, 8, own_patches, PX).transpose(2, 1, 0, 3)]
    unnamed x13 -> x25, local copies, waits for them, and re-layouts: 3.62 us -> 4.05 us
where the time goes in v6:
time: 115 us
  Pallas kernels  103 us (90%)
  local copies, waits for them, and re-layouts  8.99 us (8%)
  other arithmetic  1.72 us (1%)
    pallas_call x1, Pallas kernels, settle(): pl.pallas_call(functools.partial(settle_kernel, spans, devices), out_shap...  46.7 us
    pallas_call x1, Pallas kernels, fetch(): pl.pallas_call(functools.partial(fetch_kernel, spans, devices), out_shape...  44.5 us
    pallas_call x1, Pallas kernels, project(): pl.pallas_call(project_kernel, out_shape=jax.ShapeDtypeStruct((rows * blo...  11.8 us
    unnamed x25, local copies, waits for them, and re-layouts  4.05 us

profile of v6, /device:TPU:0, one launch (start us, length us, event | category | flops | bytes accessed | tf_op | source)
XLA Modules:
  0.0 114.7 jit_solution(11703860067006168358)
XLA Ops:
  0.6 0.8 copy.27
  1.4 0.1 reshape.131
  1.5 0.2 convert_reduce_fusion
  1.7 0.1 select_reduce_fusion
  1.9 1.5 %reshape.133 = f32[2,8,128,64]{3,2,1,0:T(8,128)S(1)} reshape(f32[16,8192]{1,0:T(8,128)} %param.11) | data formatting | bytes 1048576 | tf_op jit(solution)/shard_map/reshape | solution.py:389
  3.5 0.3 copy.28
  3.8 0.2 copy.29.table_ref.way_ref
  4.1 44.5 %shard_map.112 = (s32[32,1,128]{2,1,0:T(1,128)S(1)}, f32[32,128,128]{2,1,0:T(8,128)S(1)}, f32[16,16,128]{2,1,0:T(8,128)S(1)}, f32[16,16,128]{2,1,0:T(8,128)S(1)}) custom-call(s32[256]{0:T(256)S(1)} %multiply_add_fusion.2.slot_ref, s32[32,1,128]{2,1,0:T(1,128)S(1)} %bitcast.20, f32[128,8,128]{2,1,0:T(8,128)S(1)} %copy.29.table_ref.way_ref, ...), custom_call_target="tpu_custom_call" | custom-call | tf_op jit(solution)/shard_map/pallas_call | solution.py:179
  48.7 1.3 %copy-done = f32[32,128,128]{2,1,0:T(8,128)} copy-done((f32[32,128,128]{2,1,0:T(8,128)}, f32[32,128,128]{2,1,0:T(8,128)S(1)}, u32[]{:S(2)}) %copy-start) | copy-done | bytes 2097176
  50.0 0.1 copy.30
  50.4 1.6 %copy-done.1 = f32[32,128,128]{2,1,0:T(8,128)S(1)} copy-done((f32[32,128,128]{2,1,0:T(8,128)S(1)}, f32[32,128,128]{2,1,0:T(8,128)}, u32[]{:S(2)}) %copy-start.1) | copy-done | bytes 2097176
  52.0 11.8 %shard_map.113.part_ref = f32[256,8,128]{2,1,0:T(8,128)S(1)} custom-call(s32[256]{0:T(256)S(1)} %multiply_add_fusion.2.slot_ref, f32[32,128,128]{2,1,0:T(8,128)S(1)} %copy-done.1, f32[16,16,128]{2,1,0:T(8,128)S(1)} %get-tuple-element.10.before_ref, f32[16,16,128]{2,1,0:T(8,128)S(1)} %get-tuple-element.11.after_ref, ...), custom_call_target="tpu_custom_call" | custom-call | tf_op jit(solution)/shard_map/pallas_call | solution.py:356
  63.9 0.1 reshape_squeeze.3.asked_ref
  64.0 0.4 reshape.137
  64.4 0.3 copy.31
  64.7 0.2 copy.34.old_ref
  65.1 0.1 copy.35.scale_ref
  65.2 46.7 %shard_map.114 = (f32[128,8,128]{2,1,0:T(8,128)S(1)}, f32[16,128]{1,0:T(8,128)S(1)}) custom-call(f32[256,8,128]{2,1,0:T(8,128)S(1)} %shard_map.113.part_ref, s32[1,256]{1,0:T(1,128)S(1)} %reshape_squeeze.3.asked_ref, f32[128,8,128]{2,1,0:T(8,128)S(1)} %copy.29.table_ref.way_ref, f32[128,8,128]{2,1,0:T(8,128)S(1)} %copy.34.old_ref, f32[128,128]{1,0:T(8,128)S(1)} %copy.35.scale_ref), custom_call_target="tpu_custom_call" | custom-call | tf_op jit(solution)/shard_map/pallas_call | solution.py:285
  111.9 0.2 copy.36
  112.2 0.3 copy.37
  112.5 0.4 reshape.140
  112.9 0.2 slice_reduce_fusion.1
  113.1 0.2 copy-done.5
  113.3 1.3 %multiply_add_fusion = (f32[16,8192]{1,0:T(8,128)}, f32[16,8192]{1,0:T(8,128)}, f32[16,8192]{1,0:T(8,128)}) fusion(f32[16,8192]{1,0:T(8,128)S(1)} %copy-done.2, f32[16]{0:T(128)S(1)} %get-tuple-element.15, f32[8192]{0:T(1024)S(1)} %copy-done.6, f32[16,8192]{1,0:T(8,128)S(1)} %copy-done.4, f32[16,8192]{1,0:T(8,128)S(1)} %reshape.140, ...), kind=kLoop, calls=%fused_computation | loop fusion | flops 917504 | bytes 3702912 | tf_op jit(solution)/shard_map/add | solution.py:422
  (34 shorter events, 0.7 us)
Async XLA Ops:
  1.9 2.1 %copy-start.7 = (s32[32,1024]{1,0:T(8,128)S(1)}, s32[32,1024]{1,0:T(8,128)}, u32[]{:S(2)}) copy-start(s32[32,1024]{1,0:T(8,128)} %param.14) | copy-start | bytes 393220
  1.9 2.1 %copy-start.8 = (f32[32,1024]{1,0:T(8,128)S(1)}, f32[32,1024]{1,0:T(8,128)}, u32[]{:S(2)}) copy-start(f32[32,1024]{1,0:T(8,128)} %param.15) | copy-start | bytes 393220
  3.4 46.6 %copy-start.10 = (f32[32]{0:T(128)S(1)}, f32[32]{0:T(128)}, u32[]{:S(2)}) copy-start(f32[32]{0:T(128)} %param.16) | copy-start | bytes 388
  3.5 46.6 %copy-start.9 = (f32[32,64]{1,0:T(8,128)S(1)}, f32[32,64]{1,0:T(8,128)}, u32[]{:S(2)}) copy-start(f32[32,64]{1,0:T(8,128)} %param.17) | copy-start | bytes 24580
  4.1 59.8 %copy-start.3 = (f32[16,8192]{1,0:T(8,128)S(1)}, f32[16,8192]{1,0:T(8,128)}, u32[]{:S(2)}) copy-start(f32[16,8192]{1,0:T(8,128)} %param.10) | copy-start | bytes 1572868
  48.7 1.3 %copy-start = (f32[32,128,128]{2,1,0:T(8,128)}, f32[32,128,128]{2,1,0:T(8,128)S(1)}, u32[]{:S(2)}) copy-start(f32[32,128,128]{2,1,0:T(8,128)S(1)} %get-tuple-element.9.line_ref) | copy-start | bytes 6291460
  50.4 1.6 %copy-start.1 = (f32[32,128,128]{2,1,0:T(8,128)S(1)}, f32[32,128,128]{2,1,0:T(8,128)}, u32[]{:S(2)}) copy-start(f32[32,128,128]{2,1,0:T(8,128)} %copy-done) | copy-start | bytes 6291460
  64.0 1.0 copy-start.6
  111.9 1.2 %copy-start.2 = (f32[16,8192]{1,0:T(8,128)S(1)}, f32[16,8192]{1,0:T(8,128)}, u32[]{:S(2)}) copy-start(f32[16,8192]{1,0:T(8,128)} %param.11) | copy-start | bytes 1572868
  111.9 1.2 %copy-start.4 = (f32[16,8192]{1,0:T(8,128)S(1)}, f32[16,8192]{1,0:T(8,128)}, u32[]{:S(2)}) copy-start(f32[16,8192]{1,0:T(8,128)} %param.10) | copy-start | bytes 1572868
  112.2 1.2 %copy-start.5 = (f32[16,8192]{1,0:T(8,128)S(1)}, f32[16,8192]{1,0:T(8,128)}, u32[]{:S(2)}) copy-start(f32[16,8192]{1,0:T(8,128)} %param.9) | copy-start | bytes 1572868
